TPU v7x, 256 devices: a whole 4x4x8 slice. The times are simulated.
256 devices in a mesh: ctx: 16 (over x_hi, y, core), head: 16 (over z, x_lo).
Axes of the slice: x: 4 (x_hi: 2, x_lo: 2; x = x_hi * 2 + x_lo), y: 4, z: 8, core: 2. Of those that a mesh axis runs over, the one named last changes fastest.
Arguments:
- queries: bfloat16 [8192, 4096], P('ctx', 'head'), may hold values from -8 to 8
- keys: bfloat16 [8192, 1024], P('ctx', 'head'), may hold values from -4 to 4
- values: bfloat16 [8192, 1024], P('ctx', 'head'), may hold values from -6 to 6
- positions: int32 [8192], P('ctx'), may hold values from 0 to 8191, as said below
- out_weight: bfloat16 [4096, 4096], P('head'), may hold values from -0.125 to 0.125
Outputs:
- mixed_t: bfloat16 [4096, 8192], P('head', 'ctx')
Inputs may be any that keep to these rules, and one draw needn't show every extreme that they name: A permutation of 0 to 8191; each aligned block of 256 rows holds 256 consecutive positions in rising order, starting at a multiple of 256.
All inputs are finite; a program needn't handle non-finite values.
Results may differ from a plain program's by a relative error of at most 0.024.
Values may be sent and summed in bfloat16 or wider, within the bound.
A program may use at most 64 MiB of HBM per device.

v0:
```python
import jax
import jax.numpy as jnp
from jax import lax
from jax.sharding import PartitionSpec as P

SCALE = 0.08838834764831845
BLOCK_ROWS = 2048


def from_partner(value, axis, distance):
    mask = 2**distance
    pairs = [(source, source ^ mask) for source in range(lax.axis_size(axis))]
    return lax.ppermute(value, axis, pairs)


def absorb_block(query_heads, query_pos, carry, key_block, value_block, pos_block):
    running_top, running_total, running_sum = carry
    scores = (
        jnp.einsum("hrd,td->hrt", query_heads, key_block, preferred_element_type=jnp.float32)
        * SCALE
    )
    visible = pos_block[None, None, :] <= query_pos[None, :, None]
    scores = jnp.where(visible, scores, jnp.float32(-1e30))
    new_top = jnp.maximum(running_top, jnp.max(scores, axis=2))
    expo = jnp.where(visible, jnp.exp(scores - new_top[:, :, None]), jnp.float32(0.0))
    fade = jnp.exp(running_top - new_top)
    new_total = running_total * fade + jnp.sum(expo, axis=2)
    update = jnp.einsum(
        "hrt,td->hrd", expo.astype(jnp.bfloat16), value_block, preferred_element_type=jnp.float32
    )
    new_sum = running_sum * fade[:, :, None] + update
    return (new_top, new_total, new_sum)


def absorb(query_heads, query_pos, carry, key_rows, value_rows, pos_rows):
    count = key_rows.shape[0]
    blocks = count // BLOCK_ROWS

    def step(state, pieces):
        return (absorb_block(query_heads, query_pos, state, pieces[0], pieces[1], pieces[2]), None)

    stacked = (
        key_rows.reshape(blocks, BLOCK_ROWS, -1),
        value_rows.reshape(blocks, BLOCK_ROWS, -1),
        pos_rows.reshape(blocks, BLOCK_ROWS),
    )
    result, unused = lax.scan(step, carry, stacked)
    return result


def join_halves(own_half, other_half, is_first):
    return jnp.where(
        is_first,
        jnp.concatenate([own_half, other_half], axis=1),
        jnp.concatenate([other_half, own_half], axis=1),
    )


def body(queries, keys, values, positions, out_weight):
    rows = queries.shape[0]
    head_size = keys.shape[1] * 2
    local_heads = queries.shape[1] // head_size
    query_heads = queries.reshape(rows, local_heads, head_size).transpose(1, 0, 2)
    is_first = lax.axis_index("head") % 2 == 0
    start_state = (
        jnp.full((local_heads, rows), -1e30, jnp.float32),
        jnp.zeros((local_heads, rows), jnp.float32),
        jnp.zeros((local_heads, rows, head_size), jnp.float32),
    )
    other_keys, other_values = from_partner((keys, values), "head", 0)
    full_keys = join_halves(keys, other_keys, is_first)
    full_values = join_halves(values, other_values, is_first)
    final_state = absorb(
        query_heads,
        positions,
        start_state,
        lax.all_gather(full_keys, "ctx", axis=0, tiled=True),
        lax.all_gather(full_values, "ctx", axis=0, tiled=True),
        lax.all_gather(positions, "ctx", axis=0, tiled=True),
    )
    running_top, running_total, running_sum = final_state
    attended = (
        (running_sum / running_total[:, :, None])
        .transpose(1, 0, 2)
        .reshape(rows, local_heads * head_size)
        .astype(jnp.bfloat16)
    )
    return lax.psum_scatter(
        lax.dot_general(
            out_weight, attended, (((0,), (1,)), ((), ())), preferred_element_type=jnp.float32
        ).astype(jnp.bfloat16),
        "head",
        scatter_dimension=0,
        tiled=True,
    )


def solution(mesh):
    in_specs = (P("ctx", "head"), P("ctx", "head"), P("ctx", "head"), P("ctx"), P("head", None))
    out_specs = P("head", "ctx")
    return jax.shard_map(body, mesh=mesh, in_specs=in_specs, out_specs=out_specs, check_vma=False)
```

profile of v0, /device:TPU:1, one launch (start us, length us, event | category | flops | bytes accessed | tf_op | source)
XLA Modules:
  0.0 305.7 jit_solution(9083038737744575936)
XLA Ops:
  6.5 0.0 copy-start
  6.5 0.0 copy-start.4
  6.5 0.0 all-gather.4.cloned.1.call-start
  6.5 2.0 collective-permute-start
  8.6 1.9 collective-permute-done
  10.4 1.6 maximum_select_fusion
  12.0 0.0 all-gather.4.cloned.1.call-update
  12.1 0.0 all-gather.6.cloned.1.call-start
  12.1 1.6 collective-permute-start.1
  13.7 1.9 collective-permute-done.1
  15.5 1.6 maximum_select_fusion.1
  17.1 0.0 all-gather.6.cloned.1.call-update
  17.2 0.0 reduce-scatter.2.cloned.1.call-start
  17.2 1.1 copy.19
  18.3 0.2 copy.21
  18.5 27.8 %all-gather = s32[16,1,512]{2,1,0:T(1,128)S(1)} all-gather(s32[1,1,512]{2,1,0:T(1,128)} %bitcast.57), channel_id=1, replica_groups=mesh['ctx'=16,'head'=16] {'ctx'}, dimensions={0}, use_global_device_ids=true | all-gather | bytes 34816 | tf_op jit(solution)/shard_map/all_gather | solution.py:79
  46.3 0.1 reduce
  46.4 22.6 %all-gather.4.cloned.1.call-done = bf16[8192,128]{0,1:T(8,128)(2,1)} async-done(((bf16[512,128]{0,1:T(8,128)(2,1)}), bf16[8192,128]{0,1:T(8,128)(2,1)}) %all-gather.4.cloned.1.call-update) | async-done | bytes 2097168 | tf_op jit(solution)/shard_map/all_gather | solution.py:77
  69.1 4.0 %copy.18 = bf16[8192,128]{1,0:T(8,128)(2,1)} copy(bf16[8192,128]{0,1:T(8,128)(2,1)} %all-gather.4.cloned.1.call-done) | data formatting | bytes 4194304 | tf_op jit(solution)/shard_map/all_gather | solution.py:77
  73.1 48.8 %all-gather.6.cloned.1.call-done = bf16[8192,128]{0,1:T(8,128)(2,1)} async-done(((bf16[512,128]{0,1:T(8,128)(2,1)}), bf16[8192,128]{0,1:T(8,128)(2,1)}) %all-gather.6.cloned.1.call-update) | async-done | bytes 2097168 | tf_op jit(solution)/shard_map/all_gather | solution.py:78
  121.9 4.1 %copy.20 = bf16[8192,128]{1,0:T(8,128)(2,1)} copy(bf16[8192,128]{0,1:T(8,128)(2,1)} %all-gather.6.cloned.1.call-done) | data formatting | bytes 4194304 | tf_op jit(solution)/shard_map/all_gather | solution.py:78
  126.0 0.0 copy-done.4
  126.0 70.7 %while.15 = (s32[]{:T(128)}, f32[2,512]{1,0:T(2,128)S(1)}, f32[2,512]{1,0:T(2,128)S(1)}, f32[2,512,128]{2,1,0:T(8,128)}, s32[4,2048]{1,0:T(4,128)S(1)}, /*index=...) while((s32[]{:T(128)}, f32[2,512]{1,0:T(2,128)S(1)}, ...), condition=%wide.region_3.4_spmd.clone, body=%wide.region_0.3_spmd.clone.sunk | while | flops 1102451712 | bytes 69561560 | solution.py:47
  126.0 0.8 broadcast_compare_fusion.2
  126.8 6.1 %fusion.36 = (f32[2,512]{1,0:T(2,128)S(1)}, f32[2048,2,512]{2,0,1:T(8,128)}) fusion(pred[512,2048]{0,1:T(8,128)(4,1)S(1)} %broadcast_compare_fusion.2, bf16[2,512,128]{2,1,0:T(8,128)(2,1)S(1)} %get-tuple-element.217, bf16[4,2048,128]{2,1,0:T(8,128)(2,1)} %get-tuple-element.216, s32[]{:T(128)} %get-tuple-element.199), kind=kOutput, calls=%fused_computation.2.clone.1 | convolution fusion | flops 543161344 | bytes 10228224 | tf_op jit(solution)/shard_map/while/body/eval_jaxpr/hrd,td->hrt/dot_general | solution.py:19
  132.8 0.0 copy-start.1
  132.8 0.0 copy-start.2
  132.9 4.7 %fusion.38 = f32[2,512]{1,0:T(2,128)S(1)} fusion(f32[2048,2,512]{2,0,1:T(8,128)} %get-tuple-element.185, f32[2,512]{1,0:T(2,128)S(1)} %fusion.37, pred[512,2048]{0,1:T(8,128)(4,1)S(1)} %broadcast_compare_fusion.2), kind=kLoop, calls=%fused_computation.4.clone.1 | loop fusion | flops 10484736 | bytes 9445376 | tf_op jit(solution)/shard_map/while/body/eval_jaxpr/reduce_sum | solution.py:27
  137.6 1.1 copy-done.1
  138.7 0.0 copy-done.2
  138.7 4.1 %fusion.40 = f32[2,512,128]{2,1,0:T(8,128)S(1)} fusion(f32[2048,2,512]{2,0,1:T(8,128)S(1)} %copy-done.1, f32[2,512]{1,0:T(2,128)S(1)} %fusion.37, pred[512,2048]{0,1:T(8,128)(4,1)S(1)} %broadcast_compare_fusion.2, f32[2,512,128]{2,1,0:T(8,128)S(1)} %copy-done.2, bf16[4,2048,128]{2,1,0:T(8,128)(2,1)} %get-tuple-element.218, s32[]{:T(128)} %get-tuple-element.199, ...), kind=kOutput, calls=%fused_computation.8.clone.1 | convolution fusion | flops 547749888 | bytes 11018753 | tf_op jit(solution)/shard_map/while/body/eval_jaxpr/hrt,td->hrd/dot_general | solution.py:28
  142.8 0.0 copy-start.3
  142.9 0.8 copy-done.3
  143.7 0.8 broadcast_compare_fusion.2
  144.5 6.1 %fusion.36 = (f32[2,512]{1,0:T(2,128)S(1)}, f32[2048,2,512]{2,0,1:T(8,128)}) fusion(pred[512,2048]{0,1:T(8,128)(4,1)S(1)} %broadcast_compare_fusion.2, bf16[2,512,128]{2,1,0:T(8,128)(2,1)S(1)} %get-tuple-element.217, bf16[4,2048,128]{2,1,0:T(8,128)(2,1)} %get-tuple-element.216, s32[]{:T(128)} %get-tuple-element.199), kind=kOutput, calls=%fused_computation.2.clone.1 | convolution fusion | flops 543161344 | bytes 10228224 | tf_op jit(solution)/shard_map/while/body/eval_jaxpr/hrd,td->hrt/dot_general | solution.py:19
  150.5 4.7 %fusion.38 = f32[2,512]{1,0:T(2,128)S(1)} fusion(f32[2048,2,512]{2,0,1:T(8,128)} %get-tuple-element.185, f32[2,512]{1,0:T(2,128)S(1)} %fusion.37, pred[512,2048]{0,1:T(8,128)(4,1)S(1)} %broadcast_compare_fusion.2), kind=kLoop, calls=%fused_computation.4.clone.1 | loop fusion | flops 10484736 | bytes 9445376 | tf_op jit(solution)/shard_map/while/body/eval_jaxpr/reduce_sum | solution.py:27
  155.3 1.1 copy-done.1
  156.4 0.0 copy-done.2
  156.4 4.1 %fusion.40 = f32[2,512,128]{2,1,0:T(8,128)S(1)} fusion(f32[2048,2,512]{2,0,1:T(8,128)S(1)} %copy-done.1, f32[2,512]{1,0:T(2,128)S(1)} %fusion.37, pred[512,2048]{0,1:T(8,128)(4,1)S(1)} %broadcast_compare_fusion.2, f32[2,512,128]{2,1,0:T(8,128)S(1)} %copy-done.2, bf16[4,2048,128]{2,1,0:T(8,128)(2,1)} %get-tuple-element.218, s32[]{:T(128)} %get-tuple-element.199, ...), kind=kOutput, calls=%fused_computation.8.clone.1 | convolution fusion | flops 547749888 | bytes 11018753 | tf_op jit(solution)/shard_map/while/body/eval_jaxpr/hrt,td->hrd/dot_general | solution.py:28
  160.5 0.0 copy-start.3
  160.5 0.8 copy-done.3
  161.4 0.8 broadcast_compare_fusion.2
  162.1 6.1 %fusion.36 = (f32[2,512]{1,0:T(2,128)S(1)}, f32[2048,2,512]{2,0,1:T(8,128)}) fusion(pred[512,2048]{0,1:T(8,128)(4,1)S(1)} %broadcast_compare_fusion.2, bf16[2,512,128]{2,1,0:T(8,128)(2,1)S(1)} %get-tuple-element.217, bf16[4,2048,128]{2,1,0:T(8,128)(2,1)} %get-tuple-element.216, s32[]{:T(128)} %get-tuple-element.199), kind=kOutput, calls=%fused_computation.2.clone.1 | convolution fusion | flops 543161344 | bytes 10228224 | tf_op jit(solution)/shard_map/while/body/eval_jaxpr/hrd,td->hrt/dot_general | solution.py:19
  168.2 4.7 %fusion.38 = f32[2,512]{1,0:T(2,128)S(1)} fusion(f32[2048,2,512]{2,0,1:T(8,128)} %get-tuple-element.185, f32[2,512]{1,0:T(2,128)S(1)} %fusion.37, pred[512,2048]{0,1:T(8,128)(4,1)S(1)} %broadcast_compare_fusion.2), kind=kLoop, calls=%fused_computation.4.clone.1 | loop fusion | flops 10484736 | bytes 9445376 | tf_op jit(solution)/shard_map/while/body/eval_jaxpr/reduce_sum | solution.py:27
  173.0 1.1 copy-done.1
  174.0 0.0 copy-done.2
  174.1 4.1 %fusion.40 = f32[2,512,128]{2,1,0:T(8,128)S(1)} fusion(f32[2048,2,512]{2,0,1:T(8,128)S(1)} %copy-done.1, f32[2,512]{1,0:T(2,128)S(1)} %fusion.37, pred[512,2048]{0,1:T(8,128)(4,1)S(1)} %broadcast_compare_fusion.2, f32[2,512,128]{2,1,0:T(8,128)S(1)} %copy-done.2, bf16[4,2048,128]{2,1,0:T(8,128)(2,1)} %get-tuple-element.218, s32[]{:T(128)} %get-tuple-element.199, ...), kind=kOutput, calls=%fused_computation.8.clone.1 | convolution fusion | flops 547749888 | bytes 11018753 | tf_op jit(solution)/shard_map/while/body/eval_jaxpr/hrt,td->hrd/dot_general | solution.py:28
  178.2 0.0 copy-start.3
  178.2 0.8 copy-done.3
  179.1 0.8 broadcast_compare_fusion.2
  179.8 6.1 %fusion.36 = (f32[2,512]{1,0:T(2,128)S(1)}, f32[2048,2,512]{2,0,1:T(8,128)}) fusion(pred[512,2048]{0,1:T(8,128)(4,1)S(1)} %broadcast_compare_fusion.2, bf16[2,512,128]{2,1,0:T(8,128)(2,1)S(1)} %get-tuple-element.217, bf16[4,2048,128]{2,1,0:T(8,128)(2,1)} %get-tuple-element.216, s32[]{:T(128)} %get-tuple-element.199), kind=kOutput, calls=%fused_computation.2.clone.1 | convolution fusion | flops 543161344 | bytes 10228224 | tf_op jit(solution)/shard_map/while/body/eval_jaxpr/hrd,td->hrt/dot_general | solution.py:19
  185.9 4.7 %fusion.38 = f32[2,512]{1,0:T(2,128)S(1)} fusion(f32[2048,2,512]{2,0,1:T(8,128)} %get-tuple-element.185, f32[2,512]{1,0:T(2,128)S(1)} %fusion.37, pred[512,2048]{0,1:T(8,128)(4,1)S(1)} %broadcast_compare_fusion.2), kind=kLoop, calls=%fused_computation.4.clone.1 | loop fusion | flops 10484736 | bytes 9445376 | tf_op jit(solution)/shard_map/while/body/eval_jaxpr/reduce_sum | solution.py:27
  190.6 1.1 copy-done.1
  191.7 0.0 copy-done.2
  191.8 4.1 %fusion.40 = f32[2,512,128]{2,1,0:T(8,128)S(1)} fusion(f32[2048,2,512]{2,0,1:T(8,128)S(1)} %copy-done.1, f32[2,512]{1,0:T(2,128)S(1)} %fusion.37, pred[512,2048]{0,1:T(8,128)(4,1)S(1)} %broadcast_compare_fusion.2, f32[2,512,128]{2,1,0:T(8,128)S(1)} %copy-done.2, bf16[4,2048,128]{2,1,0:T(8,128)(2,1)} %get-tuple-element.218, s32[]{:T(128)} %get-tuple-element.199, ...), kind=kOutput, calls=%fused_computation.8.clone.1 | convolution fusion | flops 547749888 | bytes 11018753 | tf_op jit(solution)/shard_map/while/body/eval_jaxpr/hrt,td->hrd/dot_general | solution.py:28
  195.9 0.0 copy-start.3
  195.9 0.8 copy-done.3
  196.7 1.2 copy.22
  198.0 0.1 divide_convert_fusion
  198.0 0.0 copy-done
  198.0 3.2 %fusion.21 = bf16[4096,512]{0,1:T(8,128)(2,1)} fusion(bf16[512,256]{0,1:T(8,128)(2,1)S(1)} %bitcast.54, bf16[256,4096]{1,0:T(8,128)(2,1)S(1)} %copy-done), kind=kOutput, calls=%fused_computation.27 | convolution fusion | flops 1075838976 | bytes 6553600 | tf_op jit(solution)/shard_map/dot_general | solution.py:89
  201.3 0.0 reduce-scatter.2.cloned.1.call-update
  201.3 96.1 %reduce-scatter.2.cloned.1.call-done = bf16[256,512]{0,1:T(8,128)(2,1)} async-done(((bf16[4096,512]{0,1:T(8,128)(2,1)}), bf16[256,512]{0,1:T(8,128)(2,1)}) %reduce-scatter.2.cloned.1.call-update) | async-done | bytes 262160 | tf_op jit(solution)/shard_map/reduce_scatter | solution.py:88
  297.4 1.8 copy.23
  (26 shorter events, 0.2 us)
Async XLA Ops:
  6.5 191.5 %copy-start = (bf16[256,4096]{1,0:T(8,128)(2,1)S(1)}, bf16[256,4096]{1,0:T(8,128)(2,1)}, u32[]{:S(2)}) copy-start(bf16[256,4096]{1,0:T(8,128)(2,1)} %param.11) | copy-start | bytes 6291460
  6.5 119.5 %copy-start.4 = (s32[512]{0:T(512)S(1)}, s32[512]{0:T(512)}, u32[]{:S(2)}) copy-start(s32[512]{0:T(512)} %param.10) | copy-start | bytes 6148
  6.5 62.5 %all-gather.4.cloned.1.call-start = ((), (), s32[]{:S(2)}) async-start(), calls=%async_computation.1 | async-start | bytes 2228224 | tf_op jit(solution)/shard_map/all_gather | solution.py:77
  6.5 3.9 %collective-permute-start = (bf16[512,64]{0,1:T(8,128)(2,1)}, bf16[512,64]{0,1:T(8,128)(2,1)S(1)}, u32[]{:S(2)}, u32[]{:S(2)}) collective-permute-start(bf16[512,64]{0,1:T(8,128)(2,1)} %param.8), channel_id=1, source_target_pairs={{0,1},{1,0},{2,3},{3,2},{4,5},{5,4},{6,7},{7,6},{8,9},{9,8},{10,11... | collective-permute-start | bytes 196616 | tf_op jit(solution)/shard_map/ppermute | solution.py:13
  12.1 109.8 %all-gather.6.cloned.1.call-start = ((), (), s32[]{:S(2)}) async-start(), calls=%async_computation.2 | async-start | bytes 2228224 | tf_op jit(solution)/shard_map/all_gather | solution.py:78
  12.1 3.4 %collective-permute-start.1 = (bf16[512,64]{0,1:T(8,128)(2,1)}, bf16[512,64]{0,1:T(8,128)(2,1)S(1)}, u32[]{:S(2)}, u32[]{:S(2)}) collective-permute-start(bf16[512,64]{0,1:T(8,128)(2,1)} %param.9), channel_id=1, source_target_pairs={{0,1},{1,0},{2,3},{3,2},{4,5},{5,4},{6,7},{7,6},{8,9},{9,8},{10,11... | collective-permute-start | bytes 196616 | tf_op jit(solution)/shard_map/ppermute | solution.py:13
  17.2 280.2 %reduce-scatter.2.cloned.1.call-start = ((), (), s32[]{:S(2)}) async-start(), calls=%async_computation.3 | async-start | bytes 4456448 | tf_op jit(solution)/shard_map/reduce_scatter | solution.py:88
  132.8 5.8 %copy-start.1 = (f32[2048,2,512]{2,0,1:T(8,128)S(1)}, f32[2048,2,512]{2,0,1:T(8,128)}, u32[]{:S(2)}) copy-start(f32[2048,2,512]{2,0,1:T(8,128)} %get-tuple-element.185) | copy-start | bytes 25165828 | tf_op jit(solution)/shard_map/while
  132.8 5.9 %copy-start.2 = (f32[2,512,128]{2,1,0:T(8,128)S(1)}, f32[2,512,128]{2,1,0:T(8,128)}, u32[]{:S(2)}) copy-start(f32[2,512,128]{2,1,0:T(8,128)} %get-tuple-element.202) | copy-start | bytes 1572868 | tf_op jit(solution)/shard_map/while
  142.8 0.8 copy-start.3
  150.5 5.8 %copy-start.1 = (f32[2048,2,512]{2,0,1:T(8,128)S(1)}, f32[2048,2,512]{2,0,1:T(8,128)}, u32[]{:S(2)}) copy-start(f32[2048,2,512]{2,0,1:T(8,128)} %get-tuple-element.185) | copy-start | bytes 25165828 | tf_op jit(solution)/shard_map/while
  150.5 5.9 %copy-start.2 = (f32[2,512,128]{2,1,0:T(8,128)S(1)}, f32[2,512,128]{2,1,0:T(8,128)}, u32[]{:S(2)}) copy-start(f32[2,512,128]{2,1,0:T(8,128)} %get-tuple-element.202) | copy-start | bytes 1572868 | tf_op jit(solution)/shard_map/while
  160.5 0.8 copy-start.3
  168.2 5.8 %copy-start.1 = (f32[2048,2,512]{2,0,1:T(8,128)S(1)}, f32[2048,2,512]{2,0,1:T(8,128)}, u32[]{:S(2)}) copy-start(f32[2048,2,512]{2,0,1:T(8,128)} %get-tuple-element.185) | copy-start | bytes 25165828 | tf_op jit(solution)/shard_map/while
  168.2 5.9 %copy-start.2 = (f32[2,512,128]{2,1,0:T(8,128)S(1)}, f32[2,512,128]{2,1,0:T(8,128)}, u32[]{:S(2)}) copy-start(f32[2,512,128]{2,1,0:T(8,128)} %get-tuple-element.202) | copy-start | bytes 1572868 | tf_op jit(solution)/shard_map/while
  178.2 0.8 copy-start.3
  185.9 5.8 %copy-start.1 = (f32[2048,2,512]{2,0,1:T(8,128)S(1)}, f32[2048,2,512]{2,0,1:T(8,128)}, u32[]{:S(2)}) copy-start(f32[2048,2,512]{2,0,1:T(8,128)} %get-tuple-element.185) | copy-start | bytes 25165828 | tf_op jit(solution)/shard_map/while
  185.9 5.9 %copy-start.2 = (f32[2,512,128]{2,1,0:T(8,128)S(1)}, f32[2,512,128]{2,1,0:T(8,128)}, u32[]{:S(2)}) copy-start(f32[2,512,128]{2,1,0:T(8,128)} %get-tuple-element.202) | copy-start | bytes 1572868 | tf_op jit(solution)/shard_map/while
  195.9 0.8 copy-start.3
Sparse Core Ops, SparseCore 0:
  12.2 56.8 all-gather.3
  71.6 50.2 all-gather.5
  201.4 95.9 reduce-scatter.1
where the time goes:
time: 308 us; the launch traced here: 306 us
  waiting for transfers between devices  171 us (56%)
  matrix products  44 us (14%)
  blocking collectives  27.8 us (9%)
  other arithmetic  25.3 us (8%)
  local copies, waits for them, and re-layouts  20.3 us (7%)
  between operations  13.2 us (4%)
  starting transfers between devices  3.68 us (1%)
    reduce_scatter x1, waiting for transfers between devices, body(): lax.psum_scatter(lax.dot_general(out_weight, attended, (((0,), (1,)), (()...  96.1 us
    all_gather x1, waiting for transfers between devices, body(): lax.all_gather(full_values, 'ctx', axis=0, tiled=True)  48.8 us
    all_gather x1, blocking collectives, body(): lax.all_gather(positions, 'ctx', axis=0, tiled=True)  27.8 us
    dot_general x4, matrix products, absorb_block(): jnp.einsum('hrd,td->hrt', query_heads, key_block, preferred_element_type=...  24.3 us
    all_gather x1, waiting for transfers between devices, body(): lax.all_gather(full_keys, 'ctx', axis=0, tiled=True)  22.6 us
    reduce_sum x4, other arithmetic, absorb_block(): new_total = running_total * fade + jnp.sum(expo, axis=2)  18.8 us
    dot_general x4, matrix products, absorb_block(): jnp.einsum('hrt,td->hrd', expo.astype(jnp.bfloat16), value_block, preferr...  16.5 us
    while x28, local copies, waits for them, and re-layouts  7.81 us
  transfers between devices with their start and end apart: 5, of which 5 were waited for; matrix products, arithmetic and copies ran while one was open for 2% of the time, Pallas kernels for 0%

commit v1 on v0

v1 whole, which is shorter than its diff:
```python
import functools

import jax
import jax.numpy as jnp
from jax import lax
from jax.experimental import pallas as pl
from jax.experimental.pallas import tpu as pltpu
from jax.sharding import PartitionSpec as P

SCALE = 0.08838834764831845
LOG2E = 1.4426950408889634
C = SCALE * LOG2E
NEG = -1e30
HIDE = 1e30
ROWS = 512
SPAN = 256
PARTS = 4
PART = ROWS // PARTS
OFFSETS = (4, 3, -3, 2, -2, 1, -1, 0)
f32 = jnp.float32
bf16 = jnp.bfloat16
MESH = pl.DeviceIdType.MESH


def kernel(
    q_ref, k_ref, v_ref, pos_ref, w_hbm, out_ref,
    kv, posb, qT, scores, top, shift, total, acc, w_own, wT, w_oth, a_own, a_oth,
    z_out, z_in, z_out4, z_in4,
    load_sem, kv_send, kv_recv, kv_cross, pos_send, pos_recv, w_send, w_recv, w_cross,
    a_send, a_recv, z_send, z_recv,
):
    ctx = lax.axis_index("ctx")
    head = lax.axis_index("head")
    core = lax.rem(ctx, 2)
    y = lax.rem(lax.div(ctx, 2), 4)
    xh = lax.div(ctx, 8)
    z = lax.div(head, 2)
    xl = lax.rem(head, 2)
    x = xh * 2 + xl

    def device(dx, dy, dz, dcore):
        nx = lax.rem(x + dx + 4, 4)
        ny = lax.rem(y + dy + 4, 4)
        nz = lax.rem(z + dz + 8, 8)
        nc = lax.rem(core + dcore, 2)
        return {"ctx": (lax.div(nx, 2) * 4 + ny) * 2 + nc, "head": nz * 2 + lax.rem(nx, 2)}

    def first(d):
        return device(core * d, (1 - core) * d, 0, 0)

    def second(d):
        return device((1 - core) * d, core * d, 0, 0)

    other_core = device(0, 0, 0, 1)
    mate = device(1 - 2 * xl, 0, 0, 0)

    def piece_of(f, s, lane):
        own = core if lane == 0 else 1 - core
        px = lax.rem(x + own * f + (1 - own) * s, 4)
        py = lax.rem(y + (1 - own) * f + own * s, 4)
        return (lax.div(px, 2) * 4 + py) * 2 + own, lax.rem(px, 2)

    def block_of(other_hi, dy, lane):
        own = core if lane == 0 else 1 - core
        bh = 1 - xh if other_hi else xh
        return (bh * 4 + lax.rem(y + dy + 4, 4)) * 2 + own

    def remote(src, dst, send_sem, recv_sem, target):
        return pltpu.make_async_remote_copy(
            src_ref=src, dst_ref=dst, send_sem=send_sem, recv_sem=recv_sem,
            device_id=target, device_id_type=MESH,
        )

    started = []

    def send(src, dst, send_sem, recv_sem, target):
        copy = remote(src, dst, send_sem, recv_sem, target)
        copy.start()
        started.append(copy)

    def arrived(dst, recv_sem):
        remote(dst, dst, load_sem.at[0], recv_sem, other_core).wait_recv()

    load = pltpu.make_async_copy(w_hbm, w_own, load_sem.at[0])
    load.start()

    barrier = pltpu.get_barrier_semaphore()
    relations = [
        (h, dy, c) for h in range(2) for dy in range(4) for c in range(2) if (h, dy, c) != (0, 0, 0)
    ]
    friends = [device(2 * h, dy, 0, c) for h, dy, c in relations]
    friends += [device(1, 0, 0, 0), device(-1, 0, 0, 0), device(0, 0, 1, 0), device(0, 0, -1, 0)]
    for friend in friends:
        pl.semaphore_signal(barrier, inc=1, device_id=friend, device_id_type=MESH)

    my_block = block_of(False, 0, 0)
    kv[my_block, xl, 0:64, :] = k_ref[...]
    kv[my_block, xl, 64:128, :] = v_ref[...]
    lane = lax.broadcasted_iota(jnp.int32, (1, 128), 1)
    posb[my_block, :, 0:128] = pos_ref[:, 0:128] - lane
    posb[my_block, :, 128:256] = pos_ref[:, SPAN : SPAN + 128] - lane
    pl.semaphore_wait(barrier, len(friends))

    sent = [0]

    def pass_on(f, s, target, f_there, s_there, half=None):
        block, side = piece_of(f, s, 0)
        view = kv.at[block, side] if half is None else kv.at[block, side, pl.ds(64 * half, 64)]
        send(view, view, kv_send.at[sent[0]],
             kv_recv.at[f_there % 4, s_there % 4, 0 if half is None else half], target)
        sent[0] += 1

    def cross(f, s):
        block, side = piece_of(f, s, 0)
        view = kv.at[block, side]
        send(view, view, kv_send.at[sent[0]], kv_cross.at[f, s], other_core)
        sent[0] += 1

    def to_second(f):
        pass_on(f, 0, second(1), f, -1)
        pass_on(f, 0, second(-1), f, 1)

    def wait_piece(f, s):
        block, side = piece_of(f, s, 0)
        if f == 2 or s == 2:
            for half in range(2):
                if f == 2 and s != 0 and s != 2:
                    continue
                arrived(kv.at[block, side, pl.ds(64 * half, 64)], kv_recv.at[f, s, half])
            if f == 2 and s != 0 and s != 2:
                arrived(kv.at[block, side], kv_recv.at[f, s, 0])
        else:
            arrived(kv.at[block, side], kv_recv.at[f, s, 0])
        if s == 0:
            if f == 3:
                to_second(f)
                pass_on(f, 0, first(1), 2, 0, half=0)
            elif f == 1:
                to_second(f)
                pass_on(f, 0, first(-1), 2, 0, half=1)
            elif f == 2:
                to_second(f)
        elif s == 3:
            pass_on(f, s, second(1), f, 2, half=0)
        elif s == 1:
            pass_on(f, s, second(-1), f, 2, half=1)
        cross(f, s)

    def wait_cross(f, s):
        block, side = piece_of(f, s, 1)
        arrived(kv.at[block, side], kv_cross.at[f, s])

    pass_on(0, 0, first(1), -1, 0)
    pass_on(0, 0, first(-1), 1, 0)
    to_second(0)
    cross(0, 0)
    for i, (h, dy, c) in enumerate(relations):
        there = relations.index((h, (4 - dy) % 4, c))
        send(posb.at[my_block], posb.at[my_block], pos_send.at[i], pos_recv.at[there],
             device(2 * h, dy, 0, c))

    for h in range(2):
        t = q_ref[:, h * 128 : (h + 1) * 128].T
        gap = jnp.zeros((64, ROWS), bf16)
        qT[h] = jnp.concatenate([t[:64], gap, t[64:], gap], axis=0)
    top[...] = jnp.full(top.shape, NEG, f32)
    total[...] = jnp.zeros(total.shape, f32)
    acc[...] = jnp.zeros(acc.shape, f32)
    load.wait()
    for tile in range(16):
        wT[tile] = w_own[:, tile * 256 : (tile + 1) * 256].T

    row_pos = pos_ref[...]

    def stage_a(n, block, own):
        par = n % 2
        k = jnp.concatenate([kv[block, 0], kv[block, 1]], axis=0).T
        starts = [
            jnp.concatenate([posb[block, :, j * 128 : (j + 1) * 128]] * 4, axis=1) for j in range(2)
        ]
        seen = [start <= row_pos for start in starts]
        if own:
            inside = lax.broadcasted_iota(jnp.int32, (SPAN, ROWS), 0)
            masks = [inside + start <= row_pos for start in starts]
        for h in range(2):
            s = jnp.dot(k, qT[h], preferred_element_type=f32)
            if own:
                s = jnp.concatenate(
                    [jnp.where(masks[j], s[j * SPAN : (j + 1) * SPAN], NEG) for j in range(2)], axis=0
                )
            scores[par, h] = s
            new = top[par, h]
            for j in range(2):
                most = jnp.max(s[j * SPAN : (j + 1) * SPAN], axis=0, keepdims=True)
                new = jnp.maximum(new, jnp.where(seen[j], most, NEG))
            top[1 - par, h] = new
            for j in range(2):
                shift[par, h, j] = new * C + jnp.where(seen[j], 0.0, HIDE)

    def stage_b(n, block):
        par = n % 2
        v = jnp.concatenate([kv[block, 0, 64:], kv[block, 1, 64:]], axis=0)
        for h in range(2):
            fade = jnp.exp2((top[par, h] - top[1 - par, h]) * C)
            expo = [
                jnp.exp2(scores[par, h, j * SPAN : (j + 1) * SPAN] * C - shift[par, h, j])
                for j in range(2)
            ]
            total[h] = total[h] * fade + (
                jnp.sum(expo[0], axis=0, keepdims=True) + jnp.sum(expo[1], axis=0, keepdims=True)
            )
            weights = jnp.concatenate(expo, axis=0).astype(bf16)
            acc[h] = acc[h] * fade + jnp.dot(v, weights, preferred_element_type=f32)

    done = []

    def absorb(other_hi, dy, which):
        n = len(done)
        block = block_of(other_hi, dy, which)
        own = n == 0
        if own:
            stage_a(n, block, True)
        else:
            stage_b_then_a(n, block)
        done.append(block)

    def stage_b_then_a(n, block):
        par = (n - 1) % 2
        for h in range(2):
            fades[h] = jnp.exp2((top[par, h] - top[1 - par, h]) * C)
        stage_a(n, block, False)
        stage_b_with(n - 1, done[n - 1])

    fades = [None, None]

    def stage_b_with(n, block):
        par = n % 2
        v = jnp.concatenate([kv[block, 0, 64:], kv[block, 1, 64:]], axis=0)
        for h in range(2):
            fade = fades[h]
            expo = [
                jnp.exp2(scores[par, h, j * SPAN : (j + 1) * SPAN] * C - shift[par, h, j])
                for j in range(2)
            ]
            total[h] = total[h] * fade + (
                jnp.sum(expo[0], axis=0, keepdims=True) + jnp.sum(expo[1], axis=0, keepdims=True)
            )
            weights = jnp.concatenate(expo, axis=0).astype(bf16)
            acc[h] = acc[h] * fade + jnp.dot(v, weights, preferred_element_type=f32)

    for f, s in ((1, 0), (3, 0), (0, 1), (0, 3)):
        wait_piece(f, s)
    absorb(False, 0, 0)
    for i, (h, dy, c) in enumerate(relations):
        block = (lax.rem(xh + h, 2) * 4 + lax.rem(y + dy, 4)) * 2 + lax.rem(core + c, 2)
        arrived(posb.at[block], pos_recv.at[i])
    wait_cross(0, 0)
    for f, s in ((1, 0), (3, 0), (0, 1), (0, 3)):
        wait_cross(f, s)
    absorb(False, 0, 1)
    for f, s in ((1, 1), (1, 3), (3, 1), (3, 3)):
        wait_piece(f, s)
    absorb(False, 1, 0)
    absorb(False, -1, 0)
    for f, s in ((2, 0), (0, 2)):
        wait_piece(f, s)
    absorb(True, 0, 0)
    for f, s in ((1, 1), (1, 3), (3, 1), (3, 3)):
        wait_cross(f, s)
    absorb(False, 1, 1)
    absorb(False, -1, 1)
    for f, s in ((2, 1), (2, 3), (1, 2), (3, 2)):
        wait_piece(f, s)
    for f, s in ((2, 0), (0, 2)):
        wait_cross(f, s)
    absorb(True, 0, 1)
    absorb(False, 2, 0)
    for j in range(2):
        for side, d in ((0, 1), (1, -1)):
            slot = 4 * j + 2 * side + core
            offset = sum(
                (jnp.where(slot == i, o, 0) for i, o in enumerate(OFFSETS)), jnp.int32(0)
            )
            tile = lax.rem(z + offset + 8, 8) * 2 + 1 - xl
            send(wT.at[tile], w_oth.at[slot], w_send.at[j, side, 0], w_recv.at[j, side],
                 device(d, 0, 0, 0))
    absorb(True, 1, 0)
    absorb(True, -1, 0)
    wait_piece(2, 2)
    for f, s in ((2, 1), (2, 3), (1, 2), (3, 2)):
        wait_cross(f, s)
    absorb(False, 2, 1)
    absorb(True, 1, 1)
    absorb(True, -1, 1)
    absorb(True, 2, 0)
    wait_cross(2, 2)
    absorb(True, 2, 1)
    last = len(done) - 1
    stage_b(last, done[last])

    for t in range(PARTS):
        cols = slice(t * PART, (t + 1) * PART)
        for h in range(2):
            a_own[t, h * 128 : (h + 1) * 128, :] = (acc[h, :, cols] / total[h, :, cols]).astype(bf16)
        send(a_own.at[t], a_oth.at[t], a_send.at[t], a_recv.at[t], mate)

    def weights_in(j):
        for side in range(2):
            slot = 4 * j + 2 * side + core
            arrived(w_oth.at[slot], w_recv.at[j, side])
            send(w_oth.at[slot], w_oth.at[slot], w_send.at[j, side, 1], w_cross.at[j, side], other_core)

    def weights_crossed(j):
        for side in range(2):
            arrived(w_oth.at[4 * j + 2 * side + 1 - core], w_cross.at[j, side])

    weights_in(0)
    weights_in(1)
    weights_crossed(0)

    def project(offset, t):
        tile = lax.rem(z + offset + 8, 8) * 2 + xl
        return jnp.dot(wT[tile], a_own[t], preferred_element_type=f32) + jnp.dot(
            w_oth[OFFSETS.index(offset)], a_oth[t], preferred_element_type=f32
        )

    for t in range(PARTS):
        arrived(a_oth.at[t], a_recv.at[t])
        part = project(4, t)
        for d, sign in ((0, 1), (1, -1)):
            z_out4[d, t] = part[d * 128 : (d + 1) * 128].astype(bf16)
            send(z_out4.at[d, t], z_in4.at[d, t], z_send.at[d, 3, t], z_recv.at[d, 3, t],
                 device(0, 0, sign, 0))
    weights_crossed(1)
    for k in (3, 2, 1):
        for t in range(PARTS):
            for d, sign in ((0, 1), (1, -1)):
                part = project(sign * k, t)
                if k == 3:
                    arrived(z_in4.at[d, t], z_recv.at[d, 3, t])
                    more = part[d * 128 : (d + 1) * 128] + z_in4[d, t].astype(f32)
                    rest = part[(1 - d) * 128 : (2 - d) * 128]
                    z_out[d, k - 1, t, d * 128 : (d + 1) * 128, :] = more.astype(bf16)
                    z_out[d, k - 1, t, (1 - d) * 128 : (2 - d) * 128, :] = rest.astype(bf16)
                else:
                    arrived(z_in.at[d, k, t], z_recv.at[d, k, t])
                    z_out[d, k - 1, t] = (part + z_in[d, k, t].astype(f32)).astype(bf16)
                send(z_out.at[d, k - 1, t], z_in.at[d, k - 1, t], z_send.at[d, k - 1, t],
                     z_recv.at[d, k - 1, t], device(0, 0, sign, 0))
    for t in range(PARTS):
        part = project(0, t)
        for d in range(2):
            arrived(z_in.at[d, 0, t], z_recv.at[d, 0, t])
        out_ref[:, t * PART : (t + 1) * PART] = (
            part + (z_in[0, 0, t].astype(f32) + z_in[1, 0, t].astype(f32))
        ).astype(bf16)
    for copy in started:
        copy.wait_send()


def body(queries, keys, values, positions, out_weight):
    vmem = pl.BlockSpec(memory_space=pltpu.VMEM)
    dma = pltpu.SemaphoreType.DMA
    return pl.pallas_call(
        kernel,
        out_shape=jax.ShapeDtypeStruct((256, ROWS), bf16),
        in_specs=[vmem, vmem, vmem, vmem, pl.BlockSpec(memory_space=pl.ANY)],
        out_specs=vmem,
        scratch_shapes=[
            pltpu.VMEM((16, 2, 128, ROWS), bf16),
            pltpu.VMEM((16, 1, 256), jnp.int32),
            pltpu.VMEM((2, 256, ROWS), bf16),
            pltpu.VMEM((2, 2, ROWS, ROWS), f32),
            pltpu.VMEM((2, 2, 1, ROWS), f32),
            pltpu.VMEM((2, 2, 2, 1, ROWS), f32),
            pltpu.VMEM((2, 1, ROWS), f32),
            pltpu.VMEM((2, 128, ROWS), f32),
            pltpu.VMEM((256, 4096), bf16),
            pltpu.VMEM((16, 256, 256), bf16),
            pltpu.VMEM((8, 256, 256), bf16),
            pltpu.VMEM((PARTS, 256, PART), bf16),
            pltpu.VMEM((PARTS, 256, PART), bf16),
            pltpu.VMEM((2, 3, PARTS, 256, PART), bf16),
            pltpu.VMEM((2, 3, PARTS, 256, PART), bf16),
            pltpu.VMEM((2, PARTS, 128, PART), bf16),
            pltpu.VMEM((2, PARTS, 128, PART), bf16),
            dma((1,)),
            dma((36,)),
            dma((4, 4, 2)),
            dma((4, 4)),
            dma((15,)),
            dma((15,)),
            dma((2, 2, 2)),
            dma((2, 2)),
            dma((2, 2)),
            dma((PARTS,)),
            dma((PARTS,)),
            dma((2, 4, PARTS)),
            dma((2, 4, PARTS)),
        ],
        compiler_params=pltpu.CompilerParams(
            collective_id=0, has_side_effects=True, vmem_limit_bytes=48 << 20
        ),
        cost_estimate=pl.CostEstimate(flops=6_000_000_000, bytes_accessed=4_000_000, transcendentals=8_400_000),
    )(queries, keys.T, values.T, positions.reshape(1, ROWS), out_weight)


def solution(mesh):
    in_specs = (P("ctx", "head"), P("ctx", "head"), P("ctx", "head"), P("ctx"), P("head", None))
    out_specs = P("head", "ctx")
    return jax.shard_map(body, mesh=mesh, in_specs=in_specs, out_specs=out_specs, check_vma=False)
```

time: 308 us -> 69.2 us (0.22)
  waiting for transfers between devices: 171 us -> 0 us
  Pallas kernels: 0 us -> 62.4 us
  matrix products: 44 us -> 0 us
  blocking collectives: 27.8 us -> 0 us
  other arithmetic: 25.3 us -> 0 us
  local copies, waits for them, and re-layouts: 20.3 us -> 5.6 us
  between operations: 13.2 us -> 0.01 us
  starting transfers between devices: 3.68 us -> 0 us
    reduce_scatter x1 -> x0, waiting for transfers between devices: 96.1 us -> none  [body(): lax.psum_scatter(lax.dot_general(out_weight, attended, (((0,), (1,)), (()...]
    all_gather x2 -> x0, waiting for transfers between devices: 71.5 us -> none  [the longest x1 48.8 us: body(): lax.all_gather(full_values, 'ctx', axis=0, tiled=True)]
    pallas_call x0 -> x1, Pallas kernels: none -> 62.4 us  [body(): pl.pallas_call(kernel, out_shape=jax.ShapeDtypeStruct((256, ROWS), bf16),...]
    dot_general x9 -> x0, matrix products: 44 us -> none  [the longest x4 24.3 us: absorb_block(): jnp.einsum('hrd,td->hrt', query_heads, key_block, preferred_element_type=...]
    all_gather x1 -> x0, blocking collectives: 27.8 us -> none  [body(): lax.all_gather(positions, 'ctx', axis=0, tiled=True)]
    reduce_sum x4 -> x0, other arithmetic: 18.8 us -> none  [absorb_block(): new_total = running_total * fade + jnp.sum(expo, axis=2)]
    while x29 -> x0, local copies, waits for them, and re-layouts: 9.05 us -> none
    all_gather x2 -> x0, local copies, waits for them, and re-layouts: 8.13 us -> none  [the longest x1 4.08 us: body(): lax.all_gather(full_values, 'ctx', axis=0, tiled=True)]
  transfers between devices with their start and end apart: 5 -> 0, of which waited for: 5 -> 0; matrix products, arithmetic and copies ran while one was open for 2% -> 0% of each run, Pallas kernels for 0% -> 0%
where the time goes in v1:
time: 69.2 us; the launch traced here: 68 us
  Pallas kernels  62.4 us (90%)
  local copies, waits for them, and re-layouts  5.6 us (8%)
    pallas_call x1, Pallas kernels, body(): pl.pallas_call(kernel, out_shape=jax.ShapeDtypeStruct((256, ROWS), bf16),...  62.4 us
    unnamed x11, local copies, waits for them, and re-layouts  5.6 us

profile of v1, /device:TPU:1, one launch (start us, length us, event | category | flops | bytes accessed | tf_op | source)
XLA Modules:
  0.0 68.0 jit_solution(8984103628974758941)
XLA Ops:
  0.0 0.0 copy-start
  0.0 1.6 %copy-done = bf16[256,4096]{1,0:T(8,128)(2,1)S(1)} copy-done((bf16[256,4096]{1,0:T(8,128)(2,1)S(1)}, bf16[256,4096]{1,0:T(8,128)(2,1)}, u32[]{:S(2)}) %copy-start) | copy-done | bytes 2097176
  1.6 0.0 copy-start.1
  1.6 0.9 %copy-done.1 = bf16[512,256]{1,0:T(8,128)(2,1)S(1)} copy-done((bf16[512,256]{1,0:T(8,128)(2,1)S(1)}, bf16[512,256]{1,0:T(8,128)(2,1)}, u32[]{:S(2)}) %copy-start.1) | copy-done | bytes 262168
  2.5 0.0 copy-start.2
  2.5 0.8 %copy-done.2 = bf16[512,64]{0,1:T(8,128)(2,1)S(1)} copy-done((bf16[512,64]{0,1:T(8,128)(2,1)S(1)}, bf16[512,64]{0,1:T(8,128)(2,1)}, u32[]{:S(2)}) %copy-start.2) | copy-done | bytes 65560
  3.4 0.0 copy-start.3
  3.4 0.8 %copy-done.3 = bf16[512,64]{0,1:T(8,128)(2,1)S(1)} copy-done((bf16[512,64]{0,1:T(8,128)(2,1)S(1)}, bf16[512,64]{0,1:T(8,128)(2,1)}, u32[]{:S(2)}) %copy-start.3) | copy-done | bytes 65560
  4.2 0.0 copy-start.4
  4.2 0.7 copy-done.4
  4.9 62.4 %shard_map.55 = bf16[256,512]{1,0:T(8,128)(2,1)S(1)} custom-call(bf16[512,256]{1,0:T(8,128)(2,1)S(1)} %copy-done.1, bf16[64,512]{1,0:T(8,128)(2,1)S(1)} %bitcast.3, bf16[64,512]{1,0:T(8,128)(2,1)S(1)} %bitcast.4, s32[1,512]{1,0:T(1,128)S(1)} %bitcast.5, bf16[256,4096]{1,0:T(8,128)(2,1)S(1)} %copy-done), custom_call_target="tpu_custom_call" | custom-call | flops 6000000000 | bytes 4000000 | tf_op jit(solution)/shard_map/pallas_call | solution.py:364
  67.3 0.7 %copy.7 = bf16[256,512]{1,0:T(8,128)(2,1)} copy(bf16[256,512]{1,0:T(8,128)(2,1)S(1)} %shard_map.55) | data formatting | bytes 524288
Async XLA Ops:
  0.0 1.6 %copy-start = (bf16[256,4096]{1,0:T(8,128)(2,1)S(1)}, bf16[256,4096]{1,0:T(8,128)(2,1)}, u32[]{:S(2)}) copy-start(bf16[256,4096]{1,0:T(8,128)(2,1)} %w_hbm.1) | copy-start | bytes 6291460
  1.6 0.9 %copy-start.1 = (bf16[512,256]{1,0:T(8,128)(2,1)S(1)}, bf16[512,256]{1,0:T(8,128)(2,1)}, u32[]{:S(2)}) copy-start(bf16[512,256]{1,0:T(8,128)(2,1)} %q_ref.1) | copy-start | bytes 786436
  2.5 0.8 %copy-start.2 = (bf16[512,64]{0,1:T(8,128)(2,1)S(1)}, bf16[512,64]{0,1:T(8,128)(2,1)}, u32[]{:S(2)}) copy-start(bf16[512,64]{0,1:T(8,128)(2,1)} %param.6) | copy-start | bytes 196612
  3.4 0.8 %copy-start.3 = (bf16[512,64]{0,1:T(8,128)(2,1)S(1)}, bf16[512,64]{0,1:T(8,128)(2,1)}, u32[]{:S(2)}) copy-start(bf16[512,64]{0,1:T(8,128)(2,1)} %param.7) | copy-start | bytes 196612
  4.2 0.7 %copy-start.4 = (s32[512]{0:T(512)S(1)}, s32[512]{0:T(512)}, u32[]{:S(2)}) copy-start(s32[512]{0:T(512)} %param.8) | copy-start | bytes 6148

commit v2 on v1

--- a/solution.py
+++ b/solution.py
@@ -23,8 +23,8 @@
 
 
 def kernel(
-    q_ref, k_ref, v_ref, pos_ref, w_hbm, out_ref,
-    kv, posb, qT, scores, top, shift, total, acc, w_own, wT, w_oth, a_own, a_oth,
+    q_hbm, k_hbm, v_hbm, pos_hbm, w_hbm, out_ref,
+    q_ref, pos_ref, out_v, kv, posb, qT, scores, top, shift, total, acc, w_own, wT, w_oth, a_own, a_oth,
     z_out, z_in, z_out4, z_in4,
     load_sem, kv_send, kv_recv, kv_cross, pos_send, pos_recv, w_send, w_recv, w_cross,
     a_send, a_recv, z_send, z_recv,
@@ -81,8 +81,19 @@
     def arrived(dst, recv_sem):
         remote(dst, dst, load_sem.at[0], recv_sem, other_core).wait_recv()
 
-    load = pltpu.make_async_copy(w_hbm, w_own, load_sem.at[0])
-    load.start()
+    loads = []
+
+    def load(src, dst):
+        copy = pltpu.make_async_copy(src, dst, load_sem.at[len(loads)])
+        copy.start()
+        loads.append(copy)
+
+    my_block = block_of(False, 0, 0)
+    load(k_hbm, kv.at[my_block, xl, pl.ds(0, 64)])
+    load(v_hbm, kv.at[my_block, xl, pl.ds(64, 64)])
+    load(pos_hbm, pos_ref)
+    load(q_hbm, q_ref)
+    load(w_hbm, w_own)
 
     barrier = pltpu.get_barrier_semaphore()
     relations = [
@@ -92,10 +103,8 @@
     friends += [device(1, 0, 0, 0), device(-1, 0, 0, 0), device(0, 0, 1, 0), device(0, 0, -1, 0)]
     for friend in friends:
         pl.semaphore_signal(barrier, inc=1, device_id=friend, device_id_type=MESH)
-
-    my_block = block_of(False, 0, 0)
-    kv[my_block, xl, 0:64, :] = k_ref[...]
-    kv[my_block, xl, 64:128, :] = v_ref[...]
+    for i in range(3):
+        loads[i].wait()
     lane = lax.broadcasted_iota(jnp.int32, (1, 128), 1)
     posb[my_block, :, 0:128] = pos_ref[:, 0:128] - lane
     posb[my_block, :, 128:256] = pos_ref[:, SPAN : SPAN + 128] - lane
@@ -122,24 +131,13 @@
 
     def wait_piece(f, s):
         block, side = piece_of(f, s, 0)
-        if f == 2 or s == 2:
+        if s == 2 or (f, s) == (2, 0):
             for half in range(2):
-                if f == 2 and s != 0 and s != 2:
-                    continue
                 arrived(kv.at[block, side, pl.ds(64 * half, 64)], kv_recv.at[f, s, half])
-            if f == 2 and s != 0 and s != 2:
-                arrived(kv.at[block, side], kv_recv.at[f, s, 0])
         else:
             arrived(kv.at[block, side], kv_recv.at[f, s, 0])
         if s == 0:
-            if f == 3:
-                to_second(f)
-                pass_on(f, 0, first(1), 2, 0, half=0)
-            elif f == 1:
-                to_second(f)
-                pass_on(f, 0, first(-1), 2, 0, half=1)
-            elif f == 2:
-                to_second(f)
+            to_second(f)
         elif s == 3:
             pass_on(f, s, second(1), f, 2, half=0)
         elif s == 1:
@@ -152,6 +150,8 @@
 
     pass_on(0, 0, first(1), -1, 0)
     pass_on(0, 0, first(-1), 1, 0)
+    pass_on(0, 0, first(2), 2, 0, half=0)
+    pass_on(0, 0, first(-2), 2, 0, half=1)
     to_second(0)
     cross(0, 0)
     for i, (h, dy, c) in enumerate(relations):
@@ -159,6 +159,31 @@
         send(posb.at[my_block], posb.at[my_block], pos_send.at[i], pos_recv.at[there],
              device(2 * h, dy, 0, c))
 
+    def weights_out(j):
+        for side, d in ((0, 1), (1, -1)):
+            slot = 4 * j + 2 * side + core
+            offset = sum(
+                (jnp.where(slot == i, o, 0) for i, o in enumerate(OFFSETS)), jnp.int32(0)
+            )
+            tile = lax.rem(z + offset + 8, 8) * 2 + 1 - xl
+            send(wT.at[tile], w_oth.at[slot], w_send.at[j, side, 0], w_recv.at[j, side],
+                 device(d, 0, 0, 0))
+
+    def weights_in(j):
+        for side in range(2):
+            slot = 4 * j + 2 * side + core
+            arrived(w_oth.at[slot], w_recv.at[j, side])
+            send(w_oth.at[slot], w_oth.at[slot], w_send.at[j, side, 1], w_cross.at[j, side], other_core)
+
+    def weights_crossed(j):
+        for side in range(2):
+            arrived(w_oth.at[4 * j + 2 * side + 1 - core], w_cross.at[j, side])
+
+    loads[4].wait()
+    for tile in range(16):
+        wT[tile] = w_own[:, tile * 256 : (tile + 1) * 256].T
+    weights_out(0)
+    loads[3].wait()
     for h in range(2):
         t = q_ref[:, h * 128 : (h + 1) * 128].T
         gap = jnp.zeros((64, ROWS), bf16)
@@ -166,9 +191,6 @@
     top[...] = jnp.full(top.shape, NEG, f32)
     total[...] = jnp.zeros(total.shape, f32)
     acc[...] = jnp.zeros(acc.shape, f32)
-    load.wait()
-    for tile in range(16):
-        wT[tile] = w_own[:, tile * 256 : (tile + 1) * 256].T
 
     row_pos = pos_ref[...]
 
@@ -248,50 +270,44 @@
             weights = jnp.concatenate(expo, axis=0).astype(bf16)
             acc[h] = acc[h] * fade + jnp.dot(v, weights, preferred_element_type=f32)
 
-    for f, s in ((1, 0), (3, 0), (0, 1), (0, 3)):
+    for f, s in ((1, 0), (3, 0), (2, 0), (0, 1), (0, 3)):
         wait_piece(f, s)
     absorb(False, 0, 0)
     for i, (h, dy, c) in enumerate(relations):
         block = (lax.rem(xh + h, 2) * 4 + lax.rem(y + dy, 4)) * 2 + lax.rem(core + c, 2)
         arrived(posb.at[block], pos_recv.at[i])
-    wait_cross(0, 0)
-    for f, s in ((1, 0), (3, 0), (0, 1), (0, 3)):
+    for f, s in ((0, 0), (1, 0), (3, 0), (0, 1), (0, 3)):
         wait_cross(f, s)
     absorb(False, 0, 1)
-    for f, s in ((1, 1), (1, 3), (3, 1), (3, 3)):
+    for f, s in ((0, 2), (1, 1), (1, 3)):
+        wait_piece(f, s)
+    absorb(True, 0, 0)
+    for f, s in ((3, 1), (3, 3)):
         wait_piece(f, s)
     absorb(False, 1, 0)
+    weights_in(0)
     absorb(False, -1, 0)
-    for f, s in ((2, 0), (0, 2)):
-        wait_piece(f, s)
-    absorb(True, 0, 0)
-    for f, s in ((1, 1), (1, 3), (3, 1), (3, 3)):
-        wait_cross(f, s)
-    absorb(False, 1, 1)
-    absorb(False, -1, 1)
-    for f, s in ((2, 1), (2, 3), (1, 2), (3, 2)):
+    for f, s in ((2, 1), (2, 3)):
         wait_piece(f, s)
     for f, s in ((2, 0), (0, 2)):
         wait_cross(f, s)
     absorb(True, 0, 1)
+    for f, s in ((1, 1), (1, 3), (3, 1), (3, 3)):
+        wait_cross(f, s)
+    absorb(False, 1, 1)
+    for f, s in ((1, 2), (3, 2)):
+        wait_piece(f, s)
+    absorb(False, -1, 1)
     absorb(False, 2, 0)
-    for j in range(2):
-        for side, d in ((0, 1), (1, -1)):
-            slot = 4 * j + 2 * side + core
-            offset = sum(
-                (jnp.where(slot == i, o, 0) for i, o in enumerate(OFFSETS)), jnp.int32(0)
-            )
-            tile = lax.rem(z + offset + 8, 8) * 2 + 1 - xl
-            send(wT.at[tile], w_oth.at[slot], w_send.at[j, side, 0], w_recv.at[j, side],
-                 device(d, 0, 0, 0))
+    wait_piece(2, 2)
     absorb(True, 1, 0)
     absorb(True, -1, 0)
-    wait_piece(2, 2)
     for f, s in ((2, 1), (2, 3), (1, 2), (3, 2)):
         wait_cross(f, s)
     absorb(False, 2, 1)
     absorb(True, 1, 1)
     absorb(True, -1, 1)
+    weights_crossed(0)
     absorb(True, 2, 0)
     wait_cross(2, 2)
     absorb(True, 2, 1)
@@ -301,22 +317,9 @@
     for t in range(PARTS):
         cols = slice(t * PART, (t + 1) * PART)
         for h in range(2):
-            a_own[t, h * 128 : (h + 1) * 128, :] = (acc[h, :, cols] / total[h, :, cols]).astype(bf16)
+            scale = 1.0 / total[h, :, cols]
+            a_own[t, h * 128 : (h + 1) * 128, :] = (acc[h, :, cols] * scale).astype(bf16)
         send(a_own.at[t], a_oth.at[t], a_send.at[t], a_recv.at[t], mate)
-
-    def weights_in(j):
-        for side in range(2):
-            slot = 4 * j + 2 * side + core
-            arrived(w_oth.at[slot], w_recv.at[j, side])
-            send(w_oth.at[slot], w_oth.at[slot], w_send.at[j, side, 1], w_cross.at[j, side], other_core)
-
-    def weights_crossed(j):
-        for side in range(2):
-            arrived(w_oth.at[4 * j + 2 * side + 1 - core], w_cross.at[j, side])
-
-    weights_in(0)
-    weights_in(1)
-    weights_crossed(0)
 
     def project(offset, t):
         tile = lax.rem(z + offset + 8, 8) * 2 + xl
@@ -331,8 +334,11 @@
             z_out4[d, t] = part[d * 128 : (d + 1) * 128].astype(bf16)
             send(z_out4.at[d, t], z_in4.at[d, t], z_send.at[d, 3, t], z_recv.at[d, 3, t],
                  device(0, 0, sign, 0))
-    weights_crossed(1)
+    weights_out(1)
     for k in (3, 2, 1):
+        if k == 2:
+            weights_in(1)
+            weights_crossed(1)
         for t in range(PARTS):
             for d, sign in ((0, 1), (1, -1)):
                 part = project(sign * k, t)
@@ -351,22 +357,27 @@
         part = project(0, t)
         for d in range(2):
             arrived(z_in.at[d, 0, t], z_recv.at[d, 0, t])
-        out_ref[:, t * PART : (t + 1) * PART] = (
-            part + (z_in[0, 0, t].astype(f32) + z_in[1, 0, t].astype(f32))
-        ).astype(bf16)
+        cols = pl.ds(t * PART, PART)
+        out_v[:, cols] = (part + (z_in[0, 0, t].astype(f32) + z_in[1, 0, t].astype(f32))).astype(bf16)
+        load(out_v.at[:, cols], out_ref.at[:, cols])
+    for copy in loads[5:]:
+        copy.wait()
     for copy in started:
         copy.wait_send()
 
 
 def body(queries, keys, values, positions, out_weight):
-    vmem = pl.BlockSpec(memory_space=pltpu.VMEM)
+    hbm = pl.BlockSpec(memory_space=pltpu.HBM)
     dma = pltpu.SemaphoreType.DMA
     return pl.pallas_call(
         kernel,
         out_shape=jax.ShapeDtypeStruct((256, ROWS), bf16),
-        in_specs=[vmem, vmem, vmem, vmem, pl.BlockSpec(memory_space=pl.ANY)],
-        out_specs=vmem,
+        in_specs=[hbm] * 5,
+        out_specs=hbm,
         scratch_shapes=[
+            pltpu.VMEM((ROWS, 256), bf16),
+            pltpu.VMEM((1, ROWS), jnp.int32),
+            pltpu.VMEM((256, ROWS), bf16),
             pltpu.VMEM((16, 2, 128, ROWS), bf16),
             pltpu.VMEM((16, 1, 256), jnp.int32),
             pltpu.VMEM((2, 256, ROWS), bf16),
@@ -384,7 +395,7 @@
             pltpu.VMEM((2, 3, PARTS, 256, PART), bf16),
             pltpu.VMEM((2, PARTS, 128, PART), bf16),
             pltpu.VMEM((2, PARTS, 128, PART), bf16),
-            dma((1,)),
+            dma((5 + PARTS,)),
             dma((36,)),
             dma((4, 4, 2)),
             dma((4, 4)),
@@ -399,7 +410,7 @@
             dma((2, 4, PARTS)),
         ],
         compiler_params=pltpu.CompilerParams(
-            collective_id=0, has_side_effects=True, vmem_limit_bytes=48 << 20
+            collective_id=0, has_side_effects=True, vmem_limit_bytes=56 << 20
         ),
         cost_estimate=pl.CostEstimate(flops=6_000_000_000, bytes_accessed=4_000_000, transcendentals=8_400_000),
     )(queries, keys.T, values.T, positions.reshape(1, ROWS), out_weight)

time: 69.2 us -> 68.3 us (0.987); the launches traced: 68 us -> 68.1 us
  Pallas kernels: 62.4 us -> 66.5 us
  local copies, waits for them, and re-layouts: 5.6 us -> 1.67 us
    pallas_call x1, Pallas kernels: 62.4 us -> 66.5 us  [body(): pl.pallas_call(kernel, out_shape=jax.ShapeDtypeStruct((256, ROWS), bf16),...]
    unnamed x11 -> x1, local copies, waits for them, and re-layouts: 5.6 us -> 1.67 us
where the time goes in v2:
time: 68.3 us; the launch traced here: 68.1 us
  Pallas kernels  66.5 us (97%)
  local copies, waits for them, and re-layouts  1.67 us (2%)
    pallas_call x1, Pallas kernels, body(): pl.pallas_call(kernel, out_shape=jax.ShapeDtypeStruct((256, ROWS), bf16),...  66.5 us
    unnamed x1, local copies, waits for them, and re-layouts  1.67 us

profile of v2, /device:TPU:1, one launch (start us, length us, event | category | flops | bytes accessed | tf_op | source)
XLA Modules:
  0.0 68.1 jit_solution(8242013552935909923)
XLA Ops:
  0.0 66.5 %shard_map.55 = bf16[256,512]{1,0:T(8,128)(2,1)} custom-call(bf16[512,256]{1,0:T(8,128)(2,1)} %q_hbm.1, bf16[64,512]{1,0:T(8,128)(2,1)} %bitcast.3, bf16[64,512]{1,0:T(8,128)(2,1)} %bitcast.4, s32[1,512]{1,0:T(1,128)} %bitcast.5, bf16[256,4096]{1,0:T(8,128)(2,1)} %w_hbm.1), custom_call_target="tpu_custom_call" | custom-call | flops 6000000000 | bytes 4000000 | tf_op jit(solution)/shard_map/pallas_call | solution.py:372
  66.5 1.7 %copy.7 = bf16[256,512]{1,0:T(8,128)(2,1)} copy(bf16[256,512]{1,0:T(8,128)(2,1)} %shard_map.55) | data formatting | bytes 524288

commit v3 on v2

--- a/solution.py
+++ b/solution.py
@@ -24,7 +24,7 @@
 
 def kernel(
     q_hbm, k_hbm, v_hbm, pos_hbm, w_hbm, out_ref,
-    q_ref, pos_ref, out_v, kv, posb, qT, scores, top, shift, total, acc, w_own, wT, w_oth, a_own, a_oth,
+    q_ref, pos_ref, kv, posb, qT, scores, top, shift, total, acc, w_own, wT, w_oth, a_own, a_oth,
     z_out, z_in, z_out4, z_in4,
     load_sem, kv_send, kv_recv, kv_cross, pos_send, pos_recv, w_send, w_recv, w_cross,
     a_send, a_recv, z_send, z_recv,
@@ -71,12 +71,11 @@
             device_id=target, device_id_type=MESH,
         )
 
-    started = []
-
     def send(src, dst, send_sem, recv_sem, target):
-        copy = remote(src, dst, send_sem, recv_sem, target)
-        copy.start()
-        started.append(copy)
+        remote(src, dst, send_sem, recv_sem, target).start()
+
+    def sent_off(src, send_sem):
+        remote(src, src, send_sem, load_sem.at[0], other_core).wait_send()
 
     def arrived(dst, recv_sem):
         remote(dst, dst, load_sem.at[0], recv_sem, other_core).wait_recv()
@@ -110,20 +109,22 @@
     posb[my_block, :, 128:256] = pos_ref[:, SPAN : SPAN + 128] - lane
     pl.semaphore_wait(barrier, len(friends))
 
-    sent = [0]
+    passed = []
+
+    def view_of(f, s, half):
+        block, side = piece_of(f, s, 0)
+        return kv.at[block, side] if half is None else kv.at[block, side, pl.ds(64 * half, 64)]
 
     def pass_on(f, s, target, f_there, s_there, half=None):
-        block, side = piece_of(f, s, 0)
-        view = kv.at[block, side] if half is None else kv.at[block, side, pl.ds(64 * half, 64)]
-        send(view, view, kv_send.at[sent[0]],
+        view = view_of(f, s, half)
+        send(view, view, kv_send.at[len(passed)],
              kv_recv.at[f_there % 4, s_there % 4, 0 if half is None else half], target)
-        sent[0] += 1
+        passed.append((f, s, half))
 
     def cross(f, s):
-        block, side = piece_of(f, s, 0)
-        view = kv.at[block, side]
-        send(view, view, kv_send.at[sent[0]], kv_cross.at[f, s], other_core)
-        sent[0] += 1
+        view = view_of(f, s, None)
+        send(view, view, kv_send.at[len(passed)], kv_cross.at[f, s], other_core)
+        passed.append((f, s, None))
 
     def to_second(f):
         pass_on(f, 0, second(1), f, -1)
@@ -182,7 +183,6 @@
     loads[4].wait()
     for tile in range(16):
         wT[tile] = w_own[:, tile * 256 : (tile + 1) * 256].T
-    weights_out(0)
     loads[3].wait()
     for h in range(2):
         t = q_ref[:, h * 128 : (h + 1) * 128].T
@@ -219,43 +219,7 @@
             for j in range(2):
                 shift[par, h, j] = new * C + jnp.where(seen[j], 0.0, HIDE)
 
-    def stage_b(n, block):
-        par = n % 2
-        v = jnp.concatenate([kv[block, 0, 64:], kv[block, 1, 64:]], axis=0)
-        for h in range(2):
-            fade = jnp.exp2((top[par, h] - top[1 - par, h]) * C)
-            expo = [
-                jnp.exp2(scores[par, h, j * SPAN : (j + 1) * SPAN] * C - shift[par, h, j])
-                for j in range(2)
-            ]
-            total[h] = total[h] * fade + (
-                jnp.sum(expo[0], axis=0, keepdims=True) + jnp.sum(expo[1], axis=0, keepdims=True)
-            )
-            weights = jnp.concatenate(expo, axis=0).astype(bf16)
-            acc[h] = acc[h] * fade + jnp.dot(v, weights, preferred_element_type=f32)
-
-    done = []
-
-    def absorb(other_hi, dy, which):
-        n = len(done)
-        block = block_of(other_hi, dy, which)
-        own = n == 0
-        if own:
-            stage_a(n, block, True)
-        else:
-            stage_b_then_a(n, block)
-        done.append(block)
-
-    def stage_b_then_a(n, block):
-        par = (n - 1) % 2
-        for h in range(2):
-            fades[h] = jnp.exp2((top[par, h] - top[1 - par, h]) * C)
-        stage_a(n, block, False)
-        stage_b_with(n - 1, done[n - 1])
-
-    fades = [None, None]
-
-    def stage_b_with(n, block):
+    def stage_b(n, block, fades):
         par = n % 2
         v = jnp.concatenate([kv[block, 0, 64:], kv[block, 1, 64:]], axis=0)
         for h in range(2):
@@ -270,49 +234,65 @@
             weights = jnp.concatenate(expo, axis=0).astype(bf16)
             acc[h] = acc[h] * fade + jnp.dot(v, weights, preferred_element_type=f32)
 
-    for f, s in ((1, 0), (3, 0), (2, 0), (0, 1), (0, 3)):
-        wait_piece(f, s)
-    absorb(False, 0, 0)
+    def fades_of(n):
+        par = n % 2
+        return [jnp.exp2((top[par, h] - top[1 - par, h]) * C) for h in range(2)]
+
+    groups = (
+        ((1, 0), (3, 0), (2, 0), (0, 1), (0, 3)),
+        ((1, 1), (1, 3)),
+        ((3, 1), (3, 3)),
+        ((2, 1), (2, 3)),
+        ((0, 2),),
+        ((1, 2),),
+        ((3, 2),),
+        ((2, 2),),
+    )
+    orders = ((0, 1, 3, 2, 4, 5, 7, 6), (0, 4, 1, 3, 5, 7, 2, 6))
+
+    def nth_block(n, which):
+        number = core if which == 0 else 1 - core
+        code = jnp.int32(0)
+        for i in range(1, 8):
+            code = code + jnp.where(n == i, orders[0][i] + number * (orders[1][i] - orders[0][i]), 0)
+        bh = lax.rem(xh + lax.div(code, 4), 2)
+        return (bh * 4 + lax.rem(y + lax.rem(code, 4), 4)) * 2 + number
+
+    def own_group(g):
+        for f, s in groups[g]:
+            wait_piece(f, s)
+        if g == 3:
+            weights_out(0)
+
+    def cross_group(g):
+        for f, s in (((0, 0),) if g == 0 else ()) + groups[g]:
+            wait_cross(f, s)
+
+    def a_beside_b(n, block, before):
+        fades = fades_of(n - 1)
+        stage_a(n, block, False)
+        stage_b(n - 1, before, fades)
+
+    own_group(0)
+    stage_a(0, my_block, True)
     for i, (h, dy, c) in enumerate(relations):
         block = (lax.rem(xh + h, 2) * 4 + lax.rem(y + dy, 4)) * 2 + lax.rem(core + c, 2)
         arrived(posb.at[block], pos_recv.at[i])
-    for f, s in ((0, 0), (1, 0), (3, 0), (0, 1), (0, 3)):
-        wait_cross(f, s)
-    absorb(False, 0, 1)
-    for f, s in ((0, 2), (1, 1), (1, 3)):
-        wait_piece(f, s)
-    absorb(True, 0, 0)
-    for f, s in ((3, 1), (3, 3)):
-        wait_piece(f, s)
-    absorb(False, 1, 0)
-    weights_in(0)
-    absorb(False, -1, 0)
-    for f, s in ((2, 1), (2, 3)):
-        wait_piece(f, s)
-    for f, s in ((2, 0), (0, 2)):
-        wait_cross(f, s)
-    absorb(True, 0, 1)
-    for f, s in ((1, 1), (1, 3), (3, 1), (3, 3)):
-        wait_cross(f, s)
-    absorb(False, 1, 1)
-    for f, s in ((1, 2), (3, 2)):
-        wait_piece(f, s)
-    absorb(False, -1, 1)
-    absorb(False, 2, 0)
-    wait_piece(2, 2)
-    absorb(True, 1, 0)
-    absorb(True, -1, 0)
-    for f, s in ((2, 1), (2, 3), (1, 2), (3, 2)):
-        wait_cross(f, s)
-    absorb(False, 2, 1)
-    absorb(True, 1, 1)
-    absorb(True, -1, 1)
-    weights_crossed(0)
-    absorb(True, 2, 0)
-    wait_cross(2, 2)
-    absorb(True, 2, 1)
-    last = len(done) - 1
-    stage_b(last, done[last])
+
+    def two_blocks(j, carry):
+        for g in range(7):
+            @pl.when(j == g)
+            def comm(g=g):
+                own_group(g + 1)
+                cross_group(g)
+        a_beside_b(1, nth_block(j, 1), nth_block(j, 0))
+        a_beside_b(2, nth_block(j + 1, 0), nth_block(j, 1))
+        return carry
+
+    lax.fori_loop(0, 7, two_blocks, 0)
+    cross_group(7)
+    a_beside_b(1, nth_block(7, 1), nth_block(7, 0))
+    stage_b(1, nth_block(7, 1), fades_of(1))
 
     for t in range(PARTS):
         cols = slice(t * PART, (t + 1) * PART)
@@ -321,49 +301,77 @@
             a_own[t, h * 128 : (h + 1) * 128, :] = (acc[h, :, cols] * scale).astype(bf16)
         send(a_own.at[t], a_oth.at[t], a_send.at[t], a_recv.at[t], mate)
 
+    weights_in(0)
+    weights_crossed(0)
+
     def project(offset, t):
         tile = lax.rem(z + offset + 8, 8) * 2 + xl
         return jnp.dot(wT[tile], a_own[t], preferred_element_type=f32) + jnp.dot(
             w_oth[OFFSETS.index(offset)], a_oth[t], preferred_element_type=f32
         )
 
-    for t in range(PARTS):
+    def up_and_down():
+        return ((0, 1), (1, -1))
+
+    def farthest(t, carry):
         arrived(a_oth.at[t], a_recv.at[t])
         part = project(4, t)
-        for d, sign in ((0, 1), (1, -1)):
+        for d, sign in up_and_down():
             z_out4[d, t] = part[d * 128 : (d + 1) * 128].astype(bf16)
             send(z_out4.at[d, t], z_in4.at[d, t], z_send.at[d, 3, t], z_recv.at[d, 3, t],
                  device(0, 0, sign, 0))
+        return carry
+
+    def third(t, carry):
+        for d, sign in up_and_down():
+            part = project(sign * 3, t)
+            arrived(z_in4.at[d, t], z_recv.at[d, 3, t])
+            more = part[d * 128 : (d + 1) * 128] + z_in4[d, t].astype(f32)
+            rest = part[(1 - d) * 128 : (2 - d) * 128]
+            z_out[d, 2, t, d * 128 : (d + 1) * 128, :] = more.astype(bf16)
+            z_out[d, 2, t, (1 - d) * 128 : (2 - d) * 128, :] = rest.astype(bf16)
+            send(z_out.at[d, 2, t], z_in.at[d, 2, t], z_send.at[d, 2, t], z_recv.at[d, 2, t],
+                 device(0, 0, sign, 0))
+        return carry
+
+    def nearer(k, t, carry):
+        for d, sign in up_and_down():
+            part = project(sign * k, t)
+            arrived(z_in.at[d, k, t], z_recv.at[d, k, t])
+            z_out[d, k - 1, t] = (part + z_in[d, k, t].astype(f32)).astype(bf16)
+            send(z_out.at[d, k - 1, t], z_in.at[d, k - 1, t], z_send.at[d, k - 1, t],
+                 z_recv.at[d, k - 1, t], device(0, 0, sign, 0))
+        return carry
+
+    lax.fori_loop(0, PARTS, farthest, 0)
     weights_out(1)
-    for k in (3, 2, 1):
-        if k == 2:
-            weights_in(1)
-            weights_crossed(1)
-        for t in range(PARTS):
-            for d, sign in ((0, 1), (1, -1)):
-                part = project(sign * k, t)
-                if k == 3:
-                    arrived(z_in4.at[d, t], z_recv.at[d, 3, t])
-                    more = part[d * 128 : (d + 1) * 128] + z_in4[d, t].astype(f32)
-                    rest = part[(1 - d) * 128 : (2 - d) * 128]
-                    z_out[d, k - 1, t, d * 128 : (d + 1) * 128, :] = more.astype(bf16)
-                    z_out[d, k - 1, t, (1 - d) * 128 : (2 - d) * 128, :] = rest.astype(bf16)
-                else:
-                    arrived(z_in.at[d, k, t], z_recv.at[d, k, t])
-                    z_out[d, k - 1, t] = (part + z_in[d, k, t].astype(f32)).astype(bf16)
-                send(z_out.at[d, k - 1, t], z_in.at[d, k - 1, t], z_send.at[d, k - 1, t],
-                     z_recv.at[d, k - 1, t], device(0, 0, sign, 0))
+    lax.fori_loop(0, PARTS, third, 0)
+    weights_in(1)
+    weights_crossed(1)
+    lax.fori_loop(0, PARTS, functools.partial(nearer, 2), 0)
+    lax.fori_loop(0, PARTS, functools.partial(nearer, 1), 0)
     for t in range(PARTS):
         part = project(0, t)
         for d in range(2):
             arrived(z_in.at[d, 0, t], z_recv.at[d, 0, t])
-        cols = pl.ds(t * PART, PART)
-        out_v[:, cols] = (part + (z_in[0, 0, t].astype(f32) + z_in[1, 0, t].astype(f32))).astype(bf16)
-        load(out_v.at[:, cols], out_ref.at[:, cols])
-    for copy in loads[5:]:
-        copy.wait()
-    for copy in started:
-        copy.wait_send()
+        out_ref[:, t * PART : (t + 1) * PART] = (
+            part + (z_in[0, 0, t].astype(f32) + z_in[1, 0, t].astype(f32))
+        ).astype(bf16)
+
+    for i, (f, s, half) in enumerate(passed):
+        sent_off(view_of(f, s, half), kv_send.at[i])
+    for i in range(len(relations)):
+        sent_off(posb.at[my_block], pos_send.at[i])
+    for j in range(2):
+        for side in range(2):
+            for leg in range(2):
+                sent_off(wT.at[0], w_send.at[j, side, leg])
+    for t in range(PARTS):
+        sent_off(a_own.at[t], a_send.at[t])
+        for d in range(2):
+            sent_off(z_out4.at[d, t], z_send.at[d, 3, t])
+            for k in range(3):
+                sent_off(z_out.at[d, k, t], z_send.at[d, k, t])
 
 
 def body(queries, keys, values, positions, out_weight):
@@ -373,11 +381,10 @@
         kernel,
         out_shape=jax.ShapeDtypeStruct((256, ROWS), bf16),
         in_specs=[hbm] * 5,
-        out_specs=hbm,
+        out_specs=pl.BlockSpec(memory_space=pltpu.VMEM),
         scratch_shapes=[
             pltpu.VMEM((ROWS, 256), bf16),
             pltpu.VMEM((1, ROWS), jnp.int32),
-            pltpu.VMEM((256, ROWS), bf16),
             pltpu.VMEM((16, 2, 128, ROWS), bf16),
             pltpu.VMEM((16, 1, 256), jnp.int32),
             pltpu.VMEM((2, 256, ROWS), bf16),
@@ -395,7 +402,7 @@
             pltpu.VMEM((2, 3, PARTS, 256, PART), bf16),
             pltpu.VMEM((2, PARTS, 128, PART), bf16),
             pltpu.VMEM((2, PARTS, 128, PART), bf16),
-            dma((5 + PARTS,)),
+            dma((5,)),
             dma((36,)),
             dma((4, 4, 2)),
             dma((4, 4)),

time: 68.3 us -> 64 us (0.937)
  Pallas kernels: 66.5 us -> 62.2 us
    pallas_call x1, Pallas kernels: 66.5 us -> 62.2 us  [body(): pl.pallas_call(kernel, out_shape=jax.ShapeDtypeStruct((256, ROWS), bf16),...]
where the time goes in v3:
time: 64 us; the launch traced here: 63.9 us
  Pallas kernels  62.2 us (97%)
  local copies, waits for them, and re-layouts  1.67 us (3%)
    pallas_call x1, Pallas kernels, body(): pl.pallas_call(kernel, out_shape=jax.ShapeDtypeStruct((256, ROWS), bf16),...  62.2 us
    unnamed x1, local copies, waits for them, and re-layouts  1.67 us

profile of v3, /device:TPU:1, one launch (start us, length us, event | category | flops | bytes accessed | tf_op | source)
XLA Modules:
  0.0 63.9 jit_solution(7309090815799114484)
XLA Ops:
  0.0 62.2 %shard_map.55 = bf16[256,512]{1,0:T(8,128)(2,1)} custom-call(bf16[512,256]{1,0:T(8,128)(2,1)} %q_hbm.1, bf16[64,512]{1,0:T(8,128)(2,1)} %bitcast.3, bf16[64,512]{1,0:T(8,128)(2,1)} %bitcast.4, s32[1,512]{1,0:T(1,128)} %bitcast.5, bf16[256,4096]{1,0:T(8,128)(2,1)} %w_hbm.1), custom_call_target="tpu_custom_call" | custom-call | flops 6000000000 | bytes 4000000 | tf_op jit(solution)/shard_map/pallas_call | solution.py:380
  62.2 1.7 %copy.7 = bf16[256,512]{1,0:T(8,128)(2,1)} copy(bf16[256,512]{1,0:T(8,128)(2,1)} %shard_map.55) | data formatting | bytes 524288

commit v4 on v3

--- a/solution.py
+++ b/solution.py
@@ -16,6 +16,7 @@
 SPAN = 256
 PARTS = 4
 PART = ROWS // PARTS
+TILE = 256
 OFFSETS = (4, 3, -3, 2, -2, 1, -1, 0)
 f32 = jnp.float32
 bf16 = jnp.bfloat16
@@ -31,39 +32,34 @@
 ):
     ctx = lax.axis_index("ctx")
     head = lax.axis_index("head")
-    core = lax.rem(ctx, 2)
-    y = lax.rem(lax.div(ctx, 2), 4)
-    xh = lax.div(ctx, 8)
-    z = lax.div(head, 2)
-    xl = lax.rem(head, 2)
+    core = ctx & 1
+    y = (ctx >> 1) & 3
+    xh = ctx >> 3
+    z = head >> 1
+    xl = head & 1
     x = xh * 2 + xl
 
     def device(dx, dy, dz, dcore):
-        nx = lax.rem(x + dx + 4, 4)
-        ny = lax.rem(y + dy + 4, 4)
-        nz = lax.rem(z + dz + 8, 8)
-        nc = lax.rem(core + dcore, 2)
-        return {"ctx": (lax.div(nx, 2) * 4 + ny) * 2 + nc, "head": nz * 2 + lax.rem(nx, 2)}
-
-    def first(d):
-        return device(core * d, (1 - core) * d, 0, 0)
-
-    def second(d):
-        return device((1 - core) * d, core * d, 0, 0)
+        nx = (x + dx) & 3
+        ny = (y + dy) & 3
+        nz = (z + dz) & 7
+        nc = (core + dcore) & 1
+        return {"ctx": ((nx >> 1) * 4 + ny) * 2 + nc, "head": nz * 2 + (nx & 1)}
+
+    firsts = {d: device(core * d, (1 - core) * d, 0, 0) for d in (-2, -1, 1, 2)}
+    seconds = {d: device((1 - core) * d, core * d, 0, 0) for d in (-1, 1)}
+    first = firsts.get
+    second = seconds.get
 
     other_core = device(0, 0, 0, 1)
     mate = device(1 - 2 * xl, 0, 0, 0)
+    along = (device(0, 0, 1, 0), device(0, 0, -1, 0))
 
     def piece_of(f, s, lane):
         own = core if lane == 0 else 1 - core
-        px = lax.rem(x + own * f + (1 - own) * s, 4)
-        py = lax.rem(y + (1 - own) * f + own * s, 4)
-        return (lax.div(px, 2) * 4 + py) * 2 + own, lax.rem(px, 2)
-
-    def block_of(other_hi, dy, lane):
-        own = core if lane == 0 else 1 - core
-        bh = 1 - xh if other_hi else xh
-        return (bh * 4 + lax.rem(y + dy + 4, 4)) * 2 + own
+        px = (x + s + own * (f - s)) & 3
+        py = (y + f + own * (s - f)) & 3
+        return ((px >> 1) * 4 + py) * 2 + own, px & 1
 
     def remote(src, dst, send_sem, recv_sem, target):
         return pltpu.make_async_remote_copy(
@@ -87,7 +83,7 @@
         copy.start()
         loads.append(copy)
 
-    my_block = block_of(False, 0, 0)
+    my_block = ctx
     load(k_hbm, kv.at[my_block, xl, pl.ds(0, 64)])
     load(v_hbm, kv.at[my_block, xl, pl.ds(64, 64)])
     load(pos_hbm, pos_ref)
@@ -166,7 +162,7 @@
             offset = sum(
                 (jnp.where(slot == i, o, 0) for i, o in enumerate(OFFSETS)), jnp.int32(0)
             )
-            tile = lax.rem(z + offset + 8, 8) * 2 + 1 - xl
+            tile = ((z + offset) & 7) * 2 + 1 - xl
             send(wT.at[tile], w_oth.at[slot], w_send.at[j, side, 0], w_recv.at[j, side],
                  device(d, 0, 0, 0))
 
@@ -194,49 +190,48 @@
 
     row_pos = pos_ref[...]
 
-    def stage_a(n, block, own):
-        par = n % 2
-        k = jnp.concatenate([kv[block, 0], kv[block, 1]], axis=0).T
-        starts = [
+    def starts_of(block):
+        return [
             jnp.concatenate([posb[block, :, j * 128 : (j + 1) * 128]] * 4, axis=1) for j in range(2)
         ]
-        seen = [start <= row_pos for start in starts]
-        if own:
-            inside = lax.broadcasted_iota(jnp.int32, (SPAN, ROWS), 0)
-            masks = [inside + start <= row_pos for start in starts]
-        for h in range(2):
-            s = jnp.dot(k, qT[h], preferred_element_type=f32)
-            if own:
-                s = jnp.concatenate(
-                    [jnp.where(masks[j], s[j * SPAN : (j + 1) * SPAN], NEG) for j in range(2)], axis=0
-                )
-            scores[par, h] = s
-            new = top[par, h]
-            for j in range(2):
-                most = jnp.max(s[j * SPAN : (j + 1) * SPAN], axis=0, keepdims=True)
-                new = jnp.maximum(new, jnp.where(seen[j], most, NEG))
-            top[1 - par, h] = new
-            for j in range(2):
-                shift[par, h, j] = new * C + jnp.where(seen[j], 0.0, HIDE)
-
-    def stage_b(n, block, fades):
+
+    def part_a(par, h, cols, k, seen, masks):
+        s = jnp.dot(k, qT[h, :, cols], preferred_element_type=f32)
+        if masks is not None:
+            s = jnp.concatenate(
+                [jnp.where(masks[j][:, cols], s[j * SPAN : (j + 1) * SPAN], NEG) for j in range(2)], axis=0
+            )
+        scores[par, h, :, cols] = s
+        new = top[par, h, :, cols]
+        for j in range(2):
+            most = jnp.max(s[j * SPAN : (j + 1) * SPAN], axis=0, keepdims=True)
+            new = jnp.maximum(new, jnp.where(seen[j][:, cols], most, NEG))
+        top[1 - par, h, :, cols] = new
+        for j in range(2):
+            shift[par, h, j, :, cols] = new * C + jnp.where(seen[j][:, cols], 0.0, HIDE)
+
+    def part_b(par, h, cols, v, fade):
+        expo = [
+            jnp.exp2(scores[par, h, j * SPAN : (j + 1) * SPAN, cols] * C - shift[par, h, j, :, cols])
+            for j in range(2)
+        ]
+        total[h, :, cols] = total[h, :, cols] * fade + (
+            jnp.sum(expo[0], axis=0, keepdims=True) + jnp.sum(expo[1], axis=0, keepdims=True)
+        )
+        more = jnp.dot(v, jnp.concatenate(expo, axis=0).astype(bf16), preferred_element_type=f32)
+        acc[h, :, cols] = acc[h, :, cols] * fade + more
+
+    tiles = [(h, slice(r * TILE, (r + 1) * TILE)) for r in range(ROWS // TILE) for h in range(2)]
+
+    def keys_of(block):
+        return jnp.concatenate([kv[block, 0], kv[block, 1]], axis=0).T
+
+    def values_of(block):
+        return jnp.concatenate([kv[block, 0, 64:], kv[block, 1, 64:]], axis=0)
+
+    def fade_of(n, h, cols):
         par = n % 2
-        v = jnp.concatenate([kv[block, 0, 64:], kv[block, 1, 64:]], axis=0)
-        for h in range(2):
-            fade = fades[h]
-            expo = [
-                jnp.exp2(scores[par, h, j * SPAN : (j + 1) * SPAN] * C - shift[par, h, j])
-                for j in range(2)
-            ]
-            total[h] = total[h] * fade + (
-                jnp.sum(expo[0], axis=0, keepdims=True) + jnp.sum(expo[1], axis=0, keepdims=True)
-            )
-            weights = jnp.concatenate(expo, axis=0).astype(bf16)
-            acc[h] = acc[h] * fade + jnp.dot(v, weights, preferred_element_type=f32)
-
-    def fades_of(n):
-        par = n % 2
-        return [jnp.exp2((top[par, h] - top[1 - par, h]) * C) for h in range(2)]
+        return jnp.exp2((top[par, h, :, cols] - top[1 - par, h, :, cols]) * C)
 
     groups = (
         ((1, 0), (3, 0), (2, 0), (0, 1), (0, 3)),
@@ -250,13 +245,12 @@
     )
     orders = ((0, 1, 3, 2, 4, 5, 7, 6), (0, 4, 1, 3, 5, 7, 2, 6))
 
+    coded = [sum(code << (3 * i) for i, code in enumerate(order)) for order in orders]
+
     def nth_block(n, which):
         number = core if which == 0 else 1 - core
-        code = jnp.int32(0)
-        for i in range(1, 8):
-            code = code + jnp.where(n == i, orders[0][i] + number * (orders[1][i] - orders[0][i]), 0)
-        bh = lax.rem(xh + lax.div(code, 4), 2)
-        return (bh * 4 + lax.rem(y + lax.rem(code, 4), 4)) * 2 + number
+        code = ((coded[0] + number * (coded[1] - coded[0])) >> (3 * n)) & 7
+        return ((((xh + (code >> 2)) & 1) * 4) + ((y + code) & 3)) * 2 + number
 
     def own_group(g):
         for f, s in groups[g]:
@@ -268,15 +262,25 @@
         for f, s in (((0, 0),) if g == 0 else ()) + groups[g]:
             wait_cross(f, s)
 
-    def a_beside_b(n, block, before):
-        fades = fades_of(n - 1)
-        stage_a(n, block, False)
-        stage_b(n - 1, before, fades)
+    def a_beside_b(n, block, before, then=None):
+        seen = [start <= row_pos for start in starts_of(block)]
+        k, v = keys_of(block), values_of(before)
+        for h, cols in tiles:
+            fade = fade_of(n - 1, h, cols)
+            part_a(n % 2, h, cols, k, seen, None)
+            part_b((n - 1) % 2, h, cols, v, fade)
+            if then is not None:
+                then(h, cols)
 
     own_group(0)
-    stage_a(0, my_block, True)
+    starts = starts_of(my_block)
+    inside = lax.broadcasted_iota(jnp.int32, (SPAN, ROWS), 0)
+    masks = [inside + start <= row_pos for start in starts]
+    own_keys = keys_of(my_block)
+    for h, cols in tiles:
+        part_a(0, h, cols, own_keys, [start <= row_pos for start in starts], masks)
     for i, (h, dy, c) in enumerate(relations):
-        block = (lax.rem(xh + h, 2) * 4 + lax.rem(y + dy, 4)) * 2 + lax.rem(core + c, 2)
+        block = (((xh + h) & 1) * 4 + ((y + dy) & 3)) * 2 + ((core + c) & 1)
         arrived(posb.at[block], pos_recv.at[i])
 
     def two_blocks(j, carry):
@@ -291,21 +295,25 @@
 
     lax.fori_loop(0, 7, two_blocks, 0)
     cross_group(7)
-    a_beside_b(1, nth_block(7, 1), nth_block(7, 0))
-    stage_b(1, nth_block(7, 1), fades_of(1))
-
-    for t in range(PARTS):
-        cols = slice(t * PART, (t + 1) * PART)
-        for h in range(2):
-            scale = 1.0 / total[h, :, cols]
-            a_own[t, h * 128 : (h + 1) * 128, :] = (acc[h, :, cols] * scale).astype(bf16)
-        send(a_own.at[t], a_oth.at[t], a_send.at[t], a_recv.at[t], mate)
+    last_values = values_of(nth_block(7, 1))
+
+    def finish(h, cols):
+        part_b(1, h, cols, last_values, fade_of(1, h, cols))
+        scale = 1.0 / total[h, :, cols]
+        done = (acc[h, :, cols] * scale).astype(bf16)
+        for i in range(TILE // PART):
+            t = cols.start // PART + i
+            a_own[t, h * 128 : (h + 1) * 128, :] = done[:, i * PART : (i + 1) * PART]
+            if h == 1:
+                send(a_own.at[t], a_oth.at[t], a_send.at[t], a_recv.at[t], mate)
+
+    a_beside_b(1, nth_block(7, 1), nth_block(7, 0), finish)
 
     weights_in(0)
     weights_crossed(0)
 
     def project(offset, t):
-        tile = lax.rem(z + offset + 8, 8) * 2 + xl
+        tile = ((z + offset) & 7) * 2 + xl
         return jnp.dot(wT[tile], a_own[t], preferred_element_type=f32) + jnp.dot(
             w_oth[OFFSETS.index(offset)], a_oth[t], preferred_element_type=f32
         )
@@ -318,8 +326,7 @@
         part = project(4, t)
         for d, sign in up_and_down():
             z_out4[d, t] = part[d * 128 : (d + 1) * 128].astype(bf16)
-            send(z_out4.at[d, t], z_in4.at[d, t], z_send.at[d, 3, t], z_recv.at[d, 3, t],
-                 device(0, 0, sign, 0))
+            send(z_out4.at[d, t], z_in4.at[d, t], z_send.at[d, 3, t], z_recv.at[d, 3, t], along[d])
         return carry
 
     def third(t, carry):
@@ -330,8 +337,7 @@
             rest = part[(1 - d) * 128 : (2 - d) * 128]
             z_out[d, 2, t, d * 128 : (d + 1) * 128, :] = more.astype(bf16)
             z_out[d, 2, t, (1 - d) * 128 : (2 - d) * 128, :] = rest.astype(bf16)
-            send(z_out.at[d, 2, t], z_in.at[d, 2, t], z_send.at[d, 2, t], z_recv.at[d, 2, t],
-                 device(0, 0, sign, 0))
+            send(z_out.at[d, 2, t], z_in.at[d, 2, t], z_send.at[d, 2, t], z_recv.at[d, 2, t], along[d])
         return carry
 
     def nearer(k, t, carry):
@@ -340,7 +346,7 @@
             arrived(z_in.at[d, k, t], z_recv.at[d, k, t])
             z_out[d, k - 1, t] = (part + z_in[d, k, t].astype(f32)).astype(bf16)
             send(z_out.at[d, k - 1, t], z_in.at[d, k - 1, t], z_send.at[d, k - 1, t],
-                 z_recv.at[d, k - 1, t], device(0, 0, sign, 0))
+                 z_recv.at[d, k - 1, t], along[d])
         return carry
 
     lax.fori_loop(0, PARTS, farthest, 0)

time: 64 us -> 62.2 us (0.972)
  Pallas kernels: 62.2 us -> 60.4 us
    pallas_call x1, Pallas kernels: 62.2 us -> 60.4 us  [body(): pl.pallas_call(kernel, out_shape=jax.ShapeDtypeStruct((256, ROWS), bf16),...]
where the time goes in v4:
time: 62.2 us; the launch traced here: 62 us
  Pallas kernels  60.4 us (97%)
  local copies, waits for them, and re-layouts  1.67 us (3%)
    pallas_call x1, Pallas kernels, body(): pl.pallas_call(kernel, out_shape=jax.ShapeDtypeStruct((256, ROWS), bf16),...  60.4 us
    unnamed x1, local copies, waits for them, and re-layouts  1.67 us

profile of v4, /device:TPU:1, one launch (start us, length us, event | category | flops | bytes accessed | tf_op | source)
XLA Modules:
  0.0 62.0 jit_solution(18081254471228934127)
XLA Ops:
  0.0 60.4 %shard_map.55 = bf16[256,512]{1,0:T(8,128)(2,1)} custom-call(bf16[512,256]{1,0:T(8,128)(2,1)} %q_hbm.1, bf16[64,512]{1,0:T(8,128)(2,1)} %bitcast.3, bf16[64,512]{1,0:T(8,128)(2,1)} %bitcast.4, s32[1,512]{1,0:T(1,128)} %bitcast.5, bf16[256,4096]{1,0:T(8,128)(2,1)} %w_hbm.1), custom_call_target="tpu_custom_call" | custom-call | flops 6000000000 | bytes 4000000 | tf_op jit(solution)/shard_map/pallas_call | solution.py:386
  60.4 1.7 %copy.7 = bf16[256,512]{1,0:T(8,128)(2,1)} copy(bf16[256,512]{1,0:T(8,128)(2,1)} %shard_map.55) | data formatting | bytes 524288

commit v5 on v4

--- a/solution.py
+++ b/solution.py
@@ -312,11 +312,19 @@
     weights_in(0)
     weights_crossed(0)
 
-    def project(offset, t):
+    def project(offset, t, rows=slice(None)):
         tile = ((z + offset) & 7) * 2 + xl
-        return jnp.dot(wT[tile], a_own[t], preferred_element_type=f32) + jnp.dot(
-            w_oth[OFFSETS.index(offset)], a_oth[t], preferred_element_type=f32
+        return jnp.dot(wT[tile, rows], a_own[t], preferred_element_type=f32) + jnp.dot(
+            w_oth[OFFSETS.index(offset), rows], a_oth[t], preferred_element_type=f32
         )
+
+    def half_rows(d):
+        return slice(d * 128, (d + 1) * 128)
+
+    def send_half(d, half, t, sem):
+        rows = pl.ds(half * 128, 128)
+        send(z_out.at[d, 2, t, rows], z_in.at[d, 2, t, rows], z_send.at[d, sem, t], z_recv.at[d, sem, t],
+             along[d])
 
     def up_and_down():
         return ((0, 1), (1, -1))
@@ -325,25 +333,29 @@
         arrived(a_oth.at[t], a_recv.at[t])
         part = project(4, t)
         for d, sign in up_and_down():
-            z_out4[d, t] = part[d * 128 : (d + 1) * 128].astype(bf16)
+            z_out4[d, t] = part[half_rows(d)].astype(bf16)
             send(z_out4.at[d, t], z_in4.at[d, t], z_send.at[d, 3, t], z_recv.at[d, 3, t], along[d])
+        for d, sign in up_and_down():
+            z_out[d, 2, t, half_rows(1 - d), :] = project(sign * 3, t, half_rows(1 - d)).astype(bf16)
+            send_half(d, 1 - d, t, 4)
         return carry
 
     def third(t, carry):
         for d, sign in up_and_down():
-            part = project(sign * 3, t)
+            part = project(sign * 3, t, half_rows(d))
             arrived(z_in4.at[d, t], z_recv.at[d, 3, t])
-            more = part[d * 128 : (d + 1) * 128] + z_in4[d, t].astype(f32)
-            rest = part[(1 - d) * 128 : (2 - d) * 128]
-            z_out[d, 2, t, d * 128 : (d + 1) * 128, :] = more.astype(bf16)
-            z_out[d, 2, t, (1 - d) * 128 : (2 - d) * 128, :] = rest.astype(bf16)
-            send(z_out.at[d, 2, t], z_in.at[d, 2, t], z_send.at[d, 2, t], z_recv.at[d, 2, t], along[d])
+            z_out[d, 2, t, half_rows(d), :] = (part + z_in4[d, t].astype(f32)).astype(bf16)
+            send_half(d, d, t, 2)
         return carry
 
     def nearer(k, t, carry):
         for d, sign in up_and_down():
             part = project(sign * k, t)
-            arrived(z_in.at[d, k, t], z_recv.at[d, k, t])
+            if k == 2:
+                arrived(z_in.at[d, 2, t, pl.ds((1 - d) * 128, 128)], z_recv.at[d, 4, t])
+                arrived(z_in.at[d, 2, t, pl.ds(d * 128, 128)], z_recv.at[d, 2, t])
+            else:
+                arrived(z_in.at[d, k, t], z_recv.at[d, k, t])
             z_out[d, k - 1, t] = (part + z_in[d, k, t].astype(f32)).astype(bf16)
             send(z_out.at[d, k - 1, t], z_in.at[d, k - 1, t], z_send.at[d, k - 1, t],
                  z_recv.at[d, k - 1, t], along[d])
@@ -376,8 +388,10 @@
         sent_off(a_own.at[t], a_send.at[t])
         for d in range(2):
             sent_off(z_out4.at[d, t], z_send.at[d, 3, t])
-            for k in range(3):
+            for k in range(2):
                 sent_off(z_out.at[d, k, t], z_send.at[d, k, t])
+            for sem in (2, 4):
+                sent_off(z_out4.at[d, t], z_send.at[d, sem, t])
 
 
 def body(queries, keys, values, positions, out_weight):
@@ -419,8 +433,8 @@
             dma((2, 2)),
             dma((PARTS,)),
             dma((PARTS,)),
-            dma((2, 4, PARTS)),
-            dma((2, 4, PARTS)),
+            dma((2, 5, PARTS)),
+            dma((2, 5, PARTS)),
         ],
         compiler_params=pltpu.CompilerParams(
             collective_id=0, has_side_effects=True, vmem_limit_bytes=56 << 20

time: 62.2 us -> 61.9 us (level)
  no operation moved by 1% of the time
where the time goes in v5:
time: 61.9 us; the launch traced here: 61.8 us
  Pallas kernels  60.1 us (97%)
  local copies, waits for them, and re-layouts  1.67 us (3%)
    pallas_call x1, Pallas kernels, body(): pl.pallas_call(kernel, out_shape=jax.ShapeDtypeStruct((256, ROWS), bf16),...  60.1 us
    unnamed x1, local copies, waits for them, and re-layouts  1.67 us

profile of v5, /device:TPU:1, one launch (start us, length us, event | category | flops | bytes accessed | tf_op | source)
XLA Modules:
  0.0 61.8 jit_solution(7226476960825317675)
XLA Ops:
  0.0 60.1 %shard_map.55 = bf16[256,512]{1,0:T(8,128)(2,1)} custom-call(bf16[512,256]{1,0:T(8,128)(2,1)} %q_hbm.1, bf16[64,512]{1,0:T(8,128)(2,1)} %bitcast.3, bf16[64,512]{1,0:T(8,128)(2,1)} %bitcast.4, s32[1,512]{1,0:T(1,128)} %bitcast.5, bf16[256,4096]{1,0:T(8,128)(2,1)} %w_hbm.1), custom_call_target="tpu_custom_call" | custom-call | flops 6000000000 | bytes 4000000 | tf_op jit(solution)/shard_map/pallas_call | solution.py:400
  60.1 1.7 %copy.7 = bf16[256,512]{1,0:T(8,128)(2,1)} copy(bf16[256,512]{1,0:T(8,128)(2,1)} %shard_map.55) | data formatting | bytes 524288

commit v6 on v5

--- a/solution.py
+++ b/solution.py
@@ -257,6 +257,8 @@
             wait_piece(f, s)
         if g == 3:
             weights_out(0)
+        if g == 5:
+            weights_out(1)
 
     def cross_group(g):
         for f, s in (((0, 0),) if g == 0 else ()) + groups[g]:
@@ -295,6 +297,7 @@
 
     lax.fori_loop(0, 7, two_blocks, 0)
     cross_group(7)
+    weights_in(0)
     last_values = values_of(nth_block(7, 1))
 
     def finish(h, cols):
@@ -309,7 +312,6 @@
 
     a_beside_b(1, nth_block(7, 1), nth_block(7, 0), finish)
 
-    weights_in(0)
     weights_crossed(0)
 
     def project(offset, t, rows=slice(None)):
@@ -362,9 +364,8 @@
         return carry
 
     lax.fori_loop(0, PARTS, farthest, 0)
-    weights_out(1)
+    weights_in(1)
     lax.fori_loop(0, PARTS, third, 0)
-    weights_in(1)
     weights_crossed(1)
     lax.fori_loop(0, PARTS, functools.partial(nearer, 2), 0)
     lax.fori_loop(0, PARTS, functools.partial(nearer, 1), 0)

time: 61.9 us -> 59.9 us (0.968)
  Pallas kernels: 60.1 us -> 58.1 us
    pallas_call x1, Pallas kernels: 60.1 us -> 58.1 us  [body(): pl.pallas_call(kernel, out_shape=jax.ShapeDtypeStruct((256, ROWS), bf16),...]
where the time goes in v6:
time: 59.9 us; the launch traced here: 59.8 us
  Pallas kernels  58.1 us (97%)
  local copies, waits for them, and re-layouts  1.67 us (3%)
    pallas_call x1, Pallas kernels, body(): pl.pallas_call(kernel, out_shape=jax.ShapeDtypeStruct((256, ROWS), bf16),...  58.1 us
    unnamed x1, local copies, waits for them, and re-layouts  1.67 us

profile of v6, /device:TPU:1, one launch (start us, length us, event | category | flops | bytes accessed | tf_op | source)
XLA Modules:
  0.0 59.8 jit_solution(10568284324878257262)
XLA Ops:
  0.0 58.1 %shard_map.55 = bf16[256,512]{1,0:T(8,128)(2,1)} custom-call(bf16[512,256]{1,0:T(8,128)(2,1)} %q_hbm.1, bf16[64,512]{1,0:T(8,128)(2,1)} %bitcast.3, bf16[64,512]{1,0:T(8,128)(2,1)} %bitcast.4, s32[1,512]{1,0:T(1,128)} %bitcast.5, bf16[256,4096]{1,0:T(8,128)(2,1)} %w_hbm.1), custom_call_target="tpu_custom_call" | custom-call | flops 6000000000 | bytes 4000000 | tf_op jit(solution)/shard_map/pallas_call | solution.py:401
  58.1 1.7 %copy.7 = bf16[256,512]{1,0:T(8,128)(2,1)} copy(bf16[256,512]{1,0:T(8,128)(2,1)} %shard_map.55) | data formatting | bytes 524288

commit v7 on v6

--- a/solution.py
+++ b/solution.py
@@ -17,6 +17,7 @@
 PARTS = 4
 PART = ROWS // PARTS
 TILE = 256
+BOTH = (2,)
 OFFSETS = (4, 3, -3, 2, -2, 1, -1, 0)
 f32 = jnp.float32
 bf16 = jnp.bfloat16
@@ -47,6 +48,7 @@
         return {"ctx": ((nx >> 1) * 4 + ny) * 2 + nc, "head": nz * 2 + (nx & 1)}
 
     firsts = {d: device(core * d, (1 - core) * d, 0, 0) for d in (-2, -1, 1, 2)}
+    second_other = {d: device((1 - core) * d, core * d, 0, 1) for d in (-1, 1)}.get
     seconds = {d: device((1 - core) * d, core * d, 0, 0) for d in (-1, 1)}
     first = firsts.get
     second = seconds.get
@@ -96,6 +98,7 @@
     ]
     friends = [device(2 * h, dy, 0, c) for h, dy, c in relations]
     friends += [device(1, 0, 0, 0), device(-1, 0, 0, 0), device(0, 0, 1, 0), device(0, 0, -1, 0)]
+    friends += [device(1, 0, 0, 1), device(-1, 0, 0, 1)]
     for friend in friends:
         pl.semaphore_signal(barrier, inc=1, device_id=friend, device_id_type=MESH)
     for i in range(3):
@@ -121,6 +124,11 @@
         view = view_of(f, s, None)
         send(view, view, kv_send.at[len(passed)], kv_cross.at[f, s], other_core)
         passed.append((f, s, None))
+
+    def to_other(f, s, target, half):
+        view = view_of(f, s, half)
+        send(view, view, kv_send.at[len(passed)], kv_cross.at[f, 2], target)
+        passed.append((f, s, half))
 
     def to_second(f):
         pass_on(f, 0, second(1), f, -1)
@@ -137,9 +145,14 @@
             to_second(f)
         elif s == 3:
             pass_on(f, s, second(1), f, 2, half=0)
+            if f in BOTH:
+                to_other(f, s, second_other(1), half=0)
         elif s == 1:
             pass_on(f, s, second(-1), f, 2, half=1)
-        cross(f, s)
+            if f in BOTH:
+                to_other(f, s, second_other(-1), half=1)
+        if s != 2 or f not in BOTH:
+            cross(f, s)
 
     def wait_cross(f, s):
         block, side = piece_of(f, s, 1)
@@ -424,7 +437,7 @@
             pltpu.VMEM((2, PARTS, 128, PART), bf16),
             pltpu.VMEM((2, PARTS, 128, PART), bf16),
             dma((5,)),
-            dma((36,)),
+            dma((36 + len(BOTH),)),
             dma((4, 4, 2)),
             dma((4, 4)),
             dma((15,)),

time: 59.9 us -> 59.2 us (0.988)
  the two profiles are of different devices: /device:TPU:1 before, /device:TPU:4 now
where the time goes in v7:
time: 59.2 us; the launch traced here: 59.1 us
  Pallas kernels  57.4 us (97%)
  local copies, waits for them, and re-layouts  1.67 us (3%)
    pallas_call x1, Pallas kernels, body(): pl.pallas_call(kernel, out_shape=jax.ShapeDtypeStruct((256, ROWS), bf16),...  57.4 us
    unnamed x1, local copies, waits for them, and re-layouts  1.67 us

profile of v7, /device:TPU:4, one launch (start us, length us, event | category | flops | bytes accessed | tf_op | source)
XLA Modules:
  0.0 59.1 jit_solution(12239240423335264457)
XLA Ops:
  0.0 57.4 %shard_map.55 = bf16[256,512]{1,0:T(8,128)(2,1)} custom-call(bf16[512,256]{1,0:T(8,128)(2,1)} %q_hbm.1, bf16[64,512]{1,0:T(8,128)(2,1)} %bitcast.3, bf16[64,512]{1,0:T(8,128)(2,1)} %bitcast.4, s32[1,512]{1,0:T(1,128)} %bitcast.5, bf16[256,4096]{1,0:T(8,128)(2,1)} %w_hbm.1), custom_call_target="tpu_custom_call" | custom-call | flops 6000000000 | bytes 4000000 | tf_op jit(solution)/shard_map/pallas_call | solution.py:414
  57.4 1.7 %copy.7 = bf16[256,512]{1,0:T(8,128)(2,1)} copy(bf16[256,512]{1,0:T(8,128)(2,1)} %shard_map.55) | data formatting | bytes 524288

commit v8 on v7

--- a/solution.py
+++ b/solution.py
@@ -302,8 +302,12 @@
         for g in range(7):
             @pl.when(j == g)
             def comm(g=g):
-                own_group(g + 1)
-                cross_group(g)
+                if g == 0:
+                    cross_group(0)
+                    own_group(1)
+                else:
+                    own_group(g + 1)
+                    cross_group(g)
         a_beside_b(1, nth_block(j, 1), nth_block(j, 0))
         a_beside_b(2, nth_block(j + 1, 0), nth_block(j, 1))
         return carry

time: 59.2 us -> 59.2 us (level)
  no operation moved by 1% of the time
where the time goes in v8:
time: 59.2 us; the launch traced here: 59 us
  Pallas kernels  57.4 us (97%)
  local copies, waits for them, and re-layouts  1.67 us (3%)
    pallas_call x1, Pallas kernels, body(): pl.pallas_call(kernel, out_shape=jax.ShapeDtypeStruct((256, ROWS), bf16),...  57.4 us
    unnamed x1, local copies, waits for them, and re-layouts  1.67 us

profile of v8, /device:TPU:4, one launch (start us, length us, event | category | flops | bytes accessed | tf_op | source)
XLA Modules:
  0.0 59.0 jit_solution(14519438594401638020)
XLA Ops:
  0.0 57.4 %shard_map.55 = bf16[256,512]{1,0:T(8,128)(2,1)} custom-call(bf16[512,256]{1,0:T(8,128)(2,1)} %q_hbm.1, bf16[64,512]{1,0:T(8,128)(2,1)} %bitcast.3, bf16[64,512]{1,0:T(8,128)(2,1)} %bitcast.4, s32[1,512]{1,0:T(1,128)} %bitcast.5, bf16[256,4096]{1,0:T(8,128)(2,1)} %w_hbm.1), custom_call_target="tpu_custom_call" | custom-call | flops 6000000000 | bytes 4000000 | tf_op jit(solution)/shard_map/pallas_call | solution.py:418
  57.4 1.7 %copy.7 = bf16[256,512]{1,0:T(8,128)(2,1)} copy(bf16[256,512]{1,0:T(8,128)(2,1)} %shard_map.55) | data formatting | bytes 524288
